TPU v7x, 128 devices: a whole 4x4x4 slice. The times are simulated.
128 devices in a mesh: ctx: 16 (over x_hi, z, core), dp: 8 (over y, x_lo).
Axes of the slice: x: 4 (x_hi: 2, x_lo: 2; x = x_hi * 2 + x_lo), y: 4, z: 4, core: 2. Of those that a mesh axis runs over, the one named last changes fastest.
Arguments:
- layer_input: bfloat16 [8, 2048, 768], P('dp', 'ctx'), may hold values from -6 to 6
- encoder_states: bfloat16 [8, 2048, 768], P('dp', 'ctx'), may hold values from -6 to 6
- cotangent: bfloat16 [8, 2048, 768], P('dp', 'ctx'), may hold values from -6 to 6
- bucket_ids: int32 [2048], replicated, may hold values from 0 to 31
- bias_table: float32 [32, 12], replicated, may hold values from -4 to 4
- gain_first: float32 [768], replicated, may hold values from 0.1 to 1.9
- gain_second: float32 [768], replicated, may hold values from 0.1 to 1.9
- gain_third: float32 [768], replicated, may hold values from 0.1 to 1.9
- self_query: bfloat16 [768, 768], P('dp'), may hold values from -0.09375 to 0.09375
- self_key: bfloat16 [768, 768], P('dp'), may hold values from -0.09375 to 0.09375
- self_value: bfloat16 [768, 768], P('dp'), may hold values from -0.21875 to 0.21875
- self_output: bfloat16 [768, 768], P('dp'), may hold values from -1.25 to 1.25
- cross_query: bfloat16 [768, 768], P('dp'), may hold values from -0.09375 to 0.09375
- cross_key: bfloat16 [768, 768], P('dp'), may hold values from -0.09375 to 0.09375
- cross_value: bfloat16 [768, 768], P('dp'), may hold values from -0.21875 to 0.21875
- cross_output: bfloat16 [768, 768], P('dp'), may hold values from -1.75 to 1.75
- gate_weight: bfloat16 [768, 2048], P('dp'), may hold values from -0.21875 to 0.21875
- up_weight: bfloat16 [768, 2048], P('dp'), may hold values from -0.21875 to 0.21875
- down_weight: bfloat16 [2048, 768], P('dp'), may hold values from -0.125 to 0.125
Outputs:
- layer_output: bfloat16 [8, 2048, 768], P('dp', 'ctx')
- grad_input: float32 [8, 2048, 768], P('dp', 'ctx')
- grad_encoder: float32 [8, 2048, 768], P('dp', 'ctx')
- grad_bias_table: float32 [32, 12], replicated
- grad_gain_first: float32 [768], replicated
- grad_gain_second: float32 [768], replicated
- grad_gain_third: float32 [768], replicated
- grad_self_query: float32 [768, 768], P('dp')
- grad_self_key: float32 [768, 768], P('dp')
- grad_self_value: float32 [768, 768], P('dp')
- grad_self_output: float32 [768, 768], P('dp')
- grad_cross_query: float32 [768, 768], P('dp')
- grad_cross_key: float32 [768, 768], P('dp')
- grad_cross_value: float32 [768, 768], P('dp')
- grad_cross_output: float32 [768, 768], P('dp')
- grad_gate_weight: float32 [768, 2048], P('dp')
- grad_up_weight: float32 [768, 2048], P('dp')
- grad_down_weight: float32 [2048, 768], P('dp')
All inputs are finite; a program needn't handle non-finite values.
Results may differ from a plain program's by a relative error of at most 0.04.
Values may be sent and summed in bfloat16 or wider, within the bound.
A program may use at most 192 MiB of HBM per device.

v0:
```python
import math

import jax
import jax.numpy as jnp
from jax import lax
from jax.sharding import PartitionSpec as P

EPSILON = 1e-06
NEGATIVE = -1e30
PRECISE = lax.Precision.HIGHEST


def rms_norm(values, gain):
    return values * lax.rsqrt(jnp.mean(values * values, axis=-1, keepdims=True) + EPSILON) * gain


def gated_gelu(gate_act, up_act):
    return jax.nn.gelu(gate_act, approximate=True) * up_act


def project(activity, weight):
    return jnp.einsum("scd,df->scf", activity, weight, preferred_element_type=jnp.float32)


def project_back(gradient, weight):
    return jnp.einsum("scf,df->scd", gradient, weight, preferred_element_type=jnp.float32)


def outer_sum(activity, gradient):
    return jnp.einsum("scd,scf->df", activity, gradient, preferred_element_type=jnp.float32)


def split_heads(activity, head_count):
    return activity.reshape(
        activity.shape[0], activity.shape[1], head_count, activity.shape[2] // head_count
    )


def join_heads(activity):
    return activity.reshape(
        activity.shape[0], activity.shape[1], activity.shape[2] * activity.shape[3]
    )


def toeplitz(vector, row_count, key_count):
    head_count, span = vector.shape
    reverse = vector[:, ::-1]
    tiled = jnp.tile(reverse, (1, row_count + 1))
    flat = tiled[:, row_count - 1 : row_count - 1 + row_count * (span - 1)]
    return flat.reshape(head_count, row_count, span - 1)[:, :, :key_count]


def diagonal_sums(block, span):
    head_count, row_count, key_count = block.shape
    widened = jnp.pad(block, ((0, 0), (0, 0), (0, span - 1 - key_count)))
    widened = widened.reshape(head_count, row_count * (span - 1))
    placed = jnp.pad(widened, ((0, 0), (row_count - 1, span + 1))).reshape(
        head_count, row_count + 1, span
    )
    return jnp.sum(placed, axis=1)[:, ::-1]


def causal_bias(bias_info, query_begin, row_count, key_begin, key_count):
    bias_pad, margin = bias_info
    span = row_count + key_count - 1
    slice_start = margin + query_begin - key_begin - (key_count - 1)
    vector = lax.dynamic_slice_in_dim(bias_pad, slice_start, span, 1)
    bias_block = toeplitz(vector, row_count, key_count)[None]
    query_pos = query_begin + jnp.arange(row_count, dtype=jnp.int32)
    key_pos = key_begin + jnp.arange(key_count, dtype=jnp.int32)
    allowed = (query_pos[:, None] >= key_pos[None, :])[None, None]
    return (bias_block, allowed, slice_start)


def make_fold(queries, query_begin, bias_info):

    def fold_step(running, pieces, begin_row):
        key_block, value_block = pieces
        row_max, row_sum, weighted = running
        scores = jnp.einsum(
            "sqhe,skhe->shqk", queries, key_block, preferred_element_type=jnp.float32
        )
        if bias_info is not None:
            bias_block, allowed, unused = causal_bias(
                bias_info, query_begin, queries.shape[1], begin_row, key_block.shape[1]
            )
            scores = jnp.where(allowed, scores + bias_block, NEGATIVE)
        new_max = jnp.maximum(row_max, jnp.max(scores, axis=-1))
        unscaled = jnp.exp(scores - new_max[..., None])
        if bias_info is not None:
            unscaled = jnp.where(allowed, unscaled, 0.0)
        row_sum = jnp.sum(unscaled, axis=-1)
        weighted = jnp.einsum(
            "shqk,skhe->shqe",
            unscaled.astype(jnp.bfloat16),
            value_block,
            preferred_element_type=jnp.float32,
        )
        return (new_max, row_sum, weighted)

    return fold_step


def finish_rows(running):
    row_max, row_sum, weighted = running
    out_heads = jnp.transpose(weighted / row_sum[..., None], (0, 2, 1, 3))
    return (out_heads, row_max + jnp.log(row_sum))


def attend_back(queries, out_heads, grad_heads, row_lse, pair, bias_info, query_begin):
    key_all, value_all = pair
    seq_count, row_count, head_count, head_size = queries.shape
    key_total = key_all.shape[1]
    block_len = math.gcd(512, key_total)
    span = row_count + block_len - 1
    delta = jnp.transpose(jnp.sum(grad_heads.astype(jnp.float32) * out_heads, axis=-1), (0, 2, 1))

    def back_step(block_index, running):
        grad_query, grad_keys, grad_values, grad_offsets = running
        begin_row = block_index * block_len
        key_block = lax.dynamic_slice_in_dim(key_all, begin_row, block_len, 1)
        value_block = lax.dynamic_slice_in_dim(value_all, begin_row, block_len, 1)
        scores = jnp.einsum(
            "sqhe,skhe->shqk", queries, key_block, preferred_element_type=jnp.float32
        )
        if bias_info is not None:
            bias_block, allowed, slice_start = causal_bias(
                bias_info, query_begin, row_count, begin_row, block_len
            )
            scores = jnp.where(allowed, scores + bias_block, NEGATIVE)
        probs = jnp.exp(scores - row_lse[..., None])
        grad_probs = jnp.einsum(
            "sqhe,skhe->shqk", grad_heads, value_block, preferred_element_type=jnp.float32
        )
        grad_scores = (probs * (grad_probs - delta[..., None])).astype(jnp.bfloat16)
        grad_query = grad_query + jnp.einsum(
            "shqk,skhe->sqhe", grad_scores, key_block, preferred_element_type=jnp.float32
        )
        key_part = jnp.einsum(
            "shqk,sqhe->skhe", grad_scores, queries, preferred_element_type=jnp.float32
        )
        value_part = jnp.einsum(
            "shqk,sqhe->skhe",
            probs.astype(jnp.bfloat16),
            grad_heads,
            preferred_element_type=jnp.float32,
        )
        grad_keys = lax.dynamic_update_slice_in_dim(grad_keys, key_part, begin_row, 1)
        grad_values = lax.dynamic_update_slice_in_dim(grad_values, value_part, begin_row, 1)
        if bias_info is not None:
            summed = jnp.sum(grad_scores.astype(jnp.float32), axis=0)
            along = diagonal_sums(summed, span)
            current = lax.dynamic_slice_in_dim(grad_offsets, slice_start, span, 1)
            grad_offsets = lax.dynamic_update_slice_in_dim(
                grad_offsets, current + along, slice_start, 1
            )
        return (grad_query, grad_keys, grad_values, grad_offsets)

    key_shape = key_all.shape
    offset_shape = bias_info[0].shape if bias_info is not None else (1,)
    initial = (
        jnp.zeros(queries.shape, jnp.float32),
        jnp.zeros(key_shape, jnp.float32),
        jnp.zeros(key_shape, jnp.float32),
        jnp.zeros(offset_shape, jnp.float32),
    )
    return lax.fori_loop(0, key_total // block_len, back_step, initial)


def body(
    layer_input,
    encoder_states,
    cotangent,
    bucket_ids,
    bias_table,
    gain_first,
    gain_second,
    gain_third,
    self_query,
    self_key,
    self_value,
    self_output,
    cross_query,
    cross_key,
    cross_value,
    cross_output,
    gate_weight,
    up_weight,
    down_weight,
):
    head_count = bias_table.shape[1]
    bucket_count = bias_table.shape[0]
    seq_count, row_count, model_width = layer_input.shape
    head_size = model_width // head_count
    weights = (
        lax.all_gather(self_query, "dp", axis=0, tiled=True),
        lax.all_gather(self_key, "dp", axis=0, tiled=True),
        lax.all_gather(self_value, "dp", axis=0, tiled=True),
        lax.all_gather(self_output, "dp", axis=0, tiled=True),
        lax.all_gather(cross_query, "dp", axis=0, tiled=True),
        lax.all_gather(cross_key, "dp", axis=0, tiled=True),
        lax.all_gather(cross_value, "dp", axis=0, tiled=True),
        lax.all_gather(cross_output, "dp", axis=0, tiled=True),
        lax.all_gather(gate_weight, "dp", axis=0, tiled=True),
        lax.all_gather(up_weight, "dp", axis=0, tiled=True),
        lax.all_gather(down_weight, "dp", axis=0, tiled=True),
    )
    position = lax.axis_index("ctx")
    query_begin = position * row_count
    distance_count = bucket_ids.shape[0]
    margin = 2 * distance_count
    table_hot = (bucket_ids[:, None] == jnp.arange(bucket_count, dtype=jnp.int32)[None, :]).astype(
        jnp.float32
    )
    bias_rows = jnp.dot(table_hot, bias_table, precision=PRECISE)
    bias_pad = jnp.pad(jnp.transpose(bias_rows), ((0, 0), (margin, margin)))
    bias_info = (bias_pad, margin)
    initial = (
        jnp.full((seq_count, head_count, row_count), NEGATIVE, jnp.float32),
        jnp.zeros((seq_count, head_count, row_count), jnp.float32),
        jnp.zeros((seq_count, head_count, row_count, head_size), jnp.float32),
    )
    residual = layer_input.astype(jnp.float32)
    normed, back_first = jax.vjp(rms_norm, residual, gain_first)
    normed_one = normed.astype(jnp.bfloat16)
    queries = split_heads(project(normed_one, weights[0]).astype(jnp.bfloat16), head_count)
    self_pair = (
        split_heads(project(normed_one, weights[1]).astype(jnp.bfloat16), head_count),
        split_heads(project(normed_one, weights[2]).astype(jnp.bfloat16), head_count),
    )
    self_fold = make_fold(queries, query_begin, bias_info)
    self_state = self_fold(
        initial,
        (
            lax.all_gather(self_pair[0], "ctx", axis=1, tiled=True),
            lax.all_gather(self_pair[1], "ctx", axis=1, tiled=True),
        ),
        jnp.int32(0),
    )
    self_heads, self_lse = finish_rows(self_state)
    attended = join_heads(self_heads).astype(jnp.bfloat16)
    middle = residual + project(attended, weights[3])
    normed, back_second = jax.vjp(rms_norm, middle, gain_second)
    normed_two = normed.astype(jnp.bfloat16)
    cross_queries = split_heads(project(normed_two, weights[4]).astype(jnp.bfloat16), head_count)
    cross_pair = (
        split_heads(project(encoder_states, weights[5]).astype(jnp.bfloat16), head_count),
        split_heads(project(encoder_states, weights[6]).astype(jnp.bfloat16), head_count),
    )
    cross_fold = make_fold(cross_queries, query_begin, None)
    cross_state = cross_fold(
        initial,
        (
            lax.all_gather(cross_pair[0], "ctx", axis=1, tiled=True),
            lax.all_gather(cross_pair[1], "ctx", axis=1, tiled=True),
        ),
        jnp.int32(0),
    )
    cross_heads, cross_lse = finish_rows(cross_state)
    crossed = join_heads(cross_heads).astype(jnp.bfloat16)
    after_cross = middle + project(crossed, weights[7])
    normed, back_third = jax.vjp(rms_norm, after_cross, gain_third)
    normed_three = normed.astype(jnp.bfloat16)
    gate_act = project(normed_three, weights[8])
    up_act = project(normed_three, weights[9])
    mixed_act, back_mix = jax.vjp(gated_gelu, gate_act, up_act)
    mixed_low = mixed_act.astype(jnp.bfloat16)
    final = after_cross + project(mixed_low, weights[10])
    layer_output = final.astype(jnp.bfloat16)
    grad_down = outer_sum(mixed_low, cotangent)
    grad_gate, grad_up = back_mix(project_back(cotangent, weights[10]))
    grad_gate = grad_gate.astype(jnp.bfloat16)
    grad_up = grad_up.astype(jnp.bfloat16)
    grad_gate_w = outer_sum(normed_three, grad_gate)
    grad_up_w = outer_sum(normed_three, grad_up)
    grad_normed = project_back(grad_gate, weights[8]) + project_back(grad_up, weights[9])
    grad_back, grad_gain_three = back_third(grad_normed)
    grad_after = cotangent.astype(jnp.float32) + grad_back
    branch_grad = grad_after.astype(jnp.bfloat16)
    grad_cout = outer_sum(crossed, branch_grad)
    grad_crossed = project_back(branch_grad, weights[7]).astype(jnp.bfloat16)
    grad_cross_heads = split_heads(grad_crossed, head_count)
    cross_all = (
        lax.all_gather(cross_pair[0], "ctx", axis=1, tiled=True),
        lax.all_gather(cross_pair[1], "ctx", axis=1, tiled=True),
    )
    cross_back = attend_back(
        cross_queries, cross_heads, grad_cross_heads, cross_lse, cross_all, None, query_begin
    )
    cross_kv_sum = (
        lax.psum_scatter(
            cross_back[1].astype(jnp.bfloat16), "ctx", scatter_dimension=1, tiled=True
        ).astype(jnp.float32),
        lax.psum_scatter(
            cross_back[2].astype(jnp.bfloat16), "ctx", scatter_dimension=1, tiled=True
        ).astype(jnp.float32),
    )
    grad_cquery = join_heads(cross_back[0]).astype(jnp.bfloat16)
    grad_ckeys = join_heads(cross_kv_sum[0]).astype(jnp.bfloat16)
    grad_cvalues = join_heads(cross_kv_sum[1]).astype(jnp.bfloat16)
    grad_cq_w = outer_sum(normed_two, grad_cquery)
    grad_ck_w = outer_sum(encoder_states, grad_ckeys)
    grad_cv_w = outer_sum(encoder_states, grad_cvalues)
    grad_encoder = project_back(grad_ckeys, weights[5]) + project_back(grad_cvalues, weights[6])
    grad_back, grad_gain_two = back_second(project_back(grad_cquery, weights[4]))
    grad_middle = grad_after + grad_back
    branch_grad = grad_middle.astype(jnp.bfloat16)
    grad_sout = outer_sum(attended, branch_grad)
    grad_attended = project_back(branch_grad, weights[3]).astype(jnp.bfloat16)
    grad_self_heads = split_heads(grad_attended, head_count)
    self_all = (
        lax.all_gather(self_pair[0], "ctx", axis=1, tiled=True),
        lax.all_gather(self_pair[1], "ctx", axis=1, tiled=True),
    )
    self_back = attend_back(
        queries, self_heads, grad_self_heads, self_lse, self_all, bias_info, query_begin
    )
    self_kv_sum = (
        lax.psum_scatter(
            self_back[1].astype(jnp.bfloat16), "ctx", scatter_dimension=1, tiled=True
        ).astype(jnp.float32),
        lax.psum_scatter(
            self_back[2].astype(jnp.bfloat16), "ctx", scatter_dimension=1, tiled=True
        ).astype(jnp.float32),
    )
    grad_queries = join_heads(self_back[0]).astype(jnp.bfloat16)
    grad_keys = join_heads(self_kv_sum[0]).astype(jnp.bfloat16)
    grad_values = join_heads(self_kv_sum[1]).astype(jnp.bfloat16)
    grad_sq_w = outer_sum(normed_one, grad_queries)
    grad_sk_w = outer_sum(normed_one, grad_keys)
    grad_sv_w = outer_sum(normed_one, grad_values)
    grad_normed = (
        project_back(grad_queries, weights[0])
        + project_back(grad_keys, weights[1])
        + project_back(grad_values, weights[2])
    )
    grad_back, grad_gain_one = back_first(grad_normed)
    grad_input = grad_middle + grad_back
    offset_grads = self_back[3][:, margin : margin + distance_count]
    local_table = jnp.transpose(jnp.dot(offset_grads, table_hot, precision=PRECISE))
    small_sums = lax.psum(
        (grad_gain_one, grad_gain_two, grad_gain_three, local_table), ("ctx", "dp")
    )
    pieces = (
        lax.psum_scatter(
            grad_sq_w.astype(jnp.bfloat16), "dp", scatter_dimension=0, tiled=True
        ).astype(jnp.float32),
        lax.psum_scatter(
            grad_sk_w.astype(jnp.bfloat16), "dp", scatter_dimension=0, tiled=True
        ).astype(jnp.float32),
        lax.psum_scatter(
            grad_sv_w.astype(jnp.bfloat16), "dp", scatter_dimension=0, tiled=True
        ).astype(jnp.float32),
        lax.psum_scatter(
            grad_sout.astype(jnp.bfloat16), "dp", scatter_dimension=0, tiled=True
        ).astype(jnp.float32),
        lax.psum_scatter(
            grad_cq_w.astype(jnp.bfloat16), "dp", scatter_dimension=0, tiled=True
        ).astype(jnp.float32),
        lax.psum_scatter(
            grad_ck_w.astype(jnp.bfloat16), "dp", scatter_dimension=0, tiled=True
        ).astype(jnp.float32),
        lax.psum_scatter(
            grad_cv_w.astype(jnp.bfloat16), "dp", scatter_dimension=0, tiled=True
        ).astype(jnp.float32),
        lax.psum_scatter(
            grad_cout.astype(jnp.bfloat16), "dp", scatter_dimension=0, tiled=True
        ).astype(jnp.float32),
        lax.psum_scatter(
            grad_gate_w.astype(jnp.bfloat16), "dp", scatter_dimension=0, tiled=True
        ).astype(jnp.float32),
        lax.psum_scatter(
            grad_up_w.astype(jnp.bfloat16), "dp", scatter_dimension=0, tiled=True
        ).astype(jnp.float32),
        lax.psum_scatter(
            grad_down.astype(jnp.bfloat16), "dp", scatter_dimension=0, tiled=True
        ).astype(jnp.float32),
    )
    shards = (
        lax.psum(pieces[0].astype(jnp.bfloat16), "ctx").astype(jnp.float32),
        lax.psum(pieces[1].astype(jnp.bfloat16), "ctx").astype(jnp.float32),
        lax.psum(pieces[2].astype(jnp.bfloat16), "ctx").astype(jnp.float32),
        lax.psum(pieces[3].astype(jnp.bfloat16), "ctx").astype(jnp.float32),
        lax.psum(pieces[4].astype(jnp.bfloat16), "ctx").astype(jnp.float32),
        lax.psum(pieces[5].astype(jnp.bfloat16), "ctx").astype(jnp.float32),
        lax.psum(pieces[6].astype(jnp.bfloat16), "ctx").astype(jnp.float32),
        lax.psum(pieces[7].astype(jnp.bfloat16), "ctx").astype(jnp.float32),
        lax.psum(pieces[8].astype(jnp.bfloat16), "ctx").astype(jnp.float32),
        lax.psum(pieces[9].astype(jnp.bfloat16), "ctx").astype(jnp.float32),
        lax.psum(pieces[10].astype(jnp.bfloat16), "ctx").astype(jnp.float32),
    )
    return (
        layer_output,
        grad_input,
        grad_encoder,
        small_sums[3],
        small_sums[0],
        small_sums[1],
        small_sums[2],
        shards[0],
        shards[1],
        shards[2],
        shards[3],
        shards[4],
        shards[5],
        shards[6],
        shards[7],
        shards[8],
        shards[9],
        shards[10],
    )


def solution(mesh):
    placed = (
        P("dp", "ctx", None),
        P("dp", "ctx", None),
        P("dp", "ctx", None),
        P(),
        P(),
        P(),
        P(),
        P(),
        P("dp", None),
        P("dp", None),
        P("dp", None),
        P("dp", None),
        P("dp", None),
        P("dp", None),
        P("dp", None),
        P("dp", None),
        P("dp", None),
        P("dp", None),
        P("dp", None),
    )
    return jax.shard_map(
        body,
        mesh=mesh,
        in_specs=placed,
        out_specs=(
            P("dp", "ctx", None),
            P("dp", "ctx", None),
            P("dp", "ctx", None),
            P(),
            P(),
            P(),
            P(),
            P("dp", None),
            P("dp", None),
            P("dp", None),
            P("dp", None),
            P("dp", None),
            P("dp", None),
            P("dp", None),
            P("dp", None),
            P("dp", None),
            P("dp", None),
            P("dp", None),
        ),
        check_vma=False,
    )
```

profile of v0, /device:TPU:1, one launch (start us, length us, event | category | flops | bytes accessed | tf_op | source)
XLA Modules:
  0.0 2053.8 jit_solution(13189302490452182971)
XLA Ops:
  51.5 39.2 %all-gather.22.cloned.1.call-done = bf16[768,768]{1,0:T(8,128)(2,1)} async-done(((bf16[96,768]{1,0:T(8,128)(2,1)}), bf16[768,768]{1,0:T(8,128)(2,1)}) %all-gather.22.cloned.1.call-update) | async-done | bytes 1179664 | tf_op jit(solution)/shard_map/all_gather | solution.py:198
  94.7 37.8 %all-gather.30.cloned.1.call-done = bf16[768,768]{1,0:T(8,128)(2,1)} async-done(((bf16[96,768]{1,0:T(8,128)(2,1)}), bf16[768,768]{1,0:T(8,128)(2,1)}) %all-gather.30.cloned.1.call-update) | async-done | bytes 1179664 | tf_op jit(solution)/shard_map/all_gather | solution.py:201
  135.1 39.2 %all-gather.34.cloned.1.call-done = bf16[768,768]{1,0:T(8,128)(2,1)} async-done(((bf16[96,768]{1,0:T(8,128)(2,1)}), bf16[768,768]{1,0:T(8,128)(2,1)}) %all-gather.34.cloned.1.call-update) | async-done | bytes 1179664 | tf_op jit(solution)/shard_map/all_gather | solution.py:202
  365.0 39.6 %all-gather.28.cloned.1.call-done = bf16[768,768]{1,0:T(8,128)(2,1)} async-done(((bf16[96,768]{1,0:T(8,128)(2,1)}), bf16[768,768]{1,0:T(8,128)(2,1)}) %all-gather.28.cloned.1.call-update) | async-done | bytes 1179664 | tf_op jit(solution)/shard_map/all_gather | solution.py:200
  407.1 57.0 %all-gather.32.cloned.1.call-done = bf16[1,2048,12,64]{1,3,2,0:T(8,128)(2,1)} async-done(((bf16[1,128,12,64]{1,3,2,0:T(8,128)(2,1)}), bf16[1,2048,12,64]{1,3,2,0:T(8,128)(2,1)}) %all-gather.32.cloned.1.call-update) | async-done | bytes 3145744 | tf_op jit(solution)/shard_map/all_gather | solution.py:254
  474.6 42.1 %all-gather.36.cloned.1.call-done = bf16[1,2048,12,64]{1,3,2,0:T(8,128)(2,1)} async-done(((bf16[1,128,12,64]{1,3,2,0:T(8,128)(2,1)}), bf16[1,2048,12,64]{1,3,2,0:T(8,128)(2,1)}) %all-gather.36.cloned.1.call-update) | async-done | bytes 3145744 | tf_op jit(solution)/shard_map/all_gather | solution.py:255
  554.7 73.8 %all-gather.40.cloned.1.call-done = bf16[768,2048]{1,0:T(8,128)(2,1)} async-done(((bf16[96,2048]{1,0:T(8,128)(2,1)}), bf16[768,2048]{1,0:T(8,128)(2,1)}) %all-gather.40.cloned.1.call-update) | async-done | bytes 3145744 | tf_op jit(solution)/shard_map/all_gather | solution.py:204
  632.0 69.1 %all-gather.42.cloned.1.call-done = bf16[768,2048]{1,0:T(8,128)(2,1)} async-done(((bf16[96,2048]{1,0:T(8,128)(2,1)}), bf16[768,2048]{1,0:T(8,128)(2,1)}) %all-gather.42.cloned.1.call-update) | async-done | bytes 3145744 | tf_op jit(solution)/shard_map/all_gather | solution.py:205
  704.5 69.1 %all-gather.44.cloned.1.call-done = bf16[2048,768]{1,0:T(8,128)(2,1)} async-done(((bf16[256,768]{1,0:T(8,128)(2,1)}), bf16[2048,768]{1,0:T(8,128)(2,1)}) %all-gather.44.cloned.1.call-update) | async-done | bytes 3145744 | tf_op jit(solution)/shard_map/all_gather | solution.py:206
  788.7 51.7 %while.42 = (s32[]{:T(128)}, f32[1,128,12,64]{1,3,2,0:T(8,128)}, bf16[1,2048,12,64]{1,3,2,0:T(8,128)(2,1)}, bf16[1,2048,12,64]{1,3,2,0:T(8,128)(2,1)}, bf16[1,20...) while((s32[]{:T(128)}, f32[1,128,12,64]{1,3,2,0:T(8,128)}, ...), condition=%wide.region_10.11_spmd.clone, body=%wide.region_9.10_spmd.clone.sunk | while | flops 508231680 | bytes 52711724 | solution.py:167
  894.4 248.8 %while.43 = (s32[]{:T(128)}, f32[1,128,12,64]{1,3,2,0:T(8,128)}, bf16[1,2048,12,64]{1,3,2,0:T(8,128)(2,1)}, bf16[1,2048,12,64]{1,3,2,0:T(8,128)(2,1)}, f32[12,10...) while((s32[]{:T(128)}, f32[1,128,12,64]{1,3,2,0:T(8,128)}, ...), condition=%wide.region_15.16_spmd.clone, body=%wide.region_13.15_spmd.clone.sunk | while | flops 511062656 | bytes 132827840 | solution.py:167
  1242.7 75.0 %reduce-scatter.48.cloned.1.call-done = bf16[128,768]{1,0:T(8,128)(2,1)} async-done(((bf16[2048,768]{1,0:T(8,128)(2,1)}), bf16[128,768]{1,0:T(8,128)(2,1)}) %reduce-scatter.48.cloned.1.call-update) | async-done | bytes 196624
  1358.1 40.9 %reduce-scatter.56.cloned.1.call-done = bf16[96,768]{1,0:T(8,128)(2,1)} async-done(((bf16[768,768]{1,0:T(8,128)(2,1)}), bf16[96,768]{1,0:T(8,128)(2,1)}) %reduce-scatter.56.cloned.1.call-update) | async-done | bytes 147472
  1400.7 41.0 %reduce-scatter.28.cloned.1.call-done = bf16[96,768]{1,0:T(8,128)(2,1)} async-done(((bf16[768,768]{1,0:T(8,128)(2,1)}), bf16[96,768]{1,0:T(8,128)(2,1)}) %reduce-scatter.28.cloned.1.call-update) | async-done | bytes 147472 | tf_op jit(solution)/shard_map/reduce_scatter | solution.py:345
  1441.7 42.7 %reduce-scatter.34.cloned.1.call-done = bf16[96,768]{1,0:T(8,128)(2,1)} async-done(((bf16[768,768]{1,0:T(8,128)(2,1)}), bf16[96,768]{1,0:T(8,128)(2,1)}) %reduce-scatter.34.cloned.1.call-update) | async-done | bytes 147472 | tf_op jit(solution)/shard_map/reduce_scatter | solution.py:354
  1484.4 42.6 %reduce-scatter.36.cloned.1.call-done = bf16[96,768]{1,0:T(8,128)(2,1)} async-done(((bf16[768,768]{1,0:T(8,128)(2,1)}), bf16[96,768]{1,0:T(8,128)(2,1)}) %reduce-scatter.36.cloned.1.call-update) | async-done | bytes 147472 | tf_op jit(solution)/shard_map/reduce_scatter | solution.py:357
  1527.0 42.9 %reduce-scatter.38.cloned.1.call-done = bf16[96,768]{1,0:T(8,128)(2,1)} async-done(((bf16[768,768]{1,0:T(8,128)(2,1)}), bf16[96,768]{1,0:T(8,128)(2,1)}) %reduce-scatter.38.cloned.1.call-update) | async-done | bytes 147472 | tf_op jit(solution)/shard_map/reduce_scatter | solution.py:366
  1569.9 77.8 %reduce-scatter.40.cloned.1.call-done = bf16[96,2048]{1,0:T(8,128)(2,1)} async-done(((bf16[768,2048]{1,0:T(8,128)(2,1)}), bf16[96,2048]{1,0:T(8,128)(2,1)}) %reduce-scatter.40.cloned.1.call-update) | async-done | bytes 393232 | tf_op jit(solution)/shard_map/reduce_scatter | solution.py:369
  1647.7 73.7 %reduce-scatter.42.cloned.1.call-done = bf16[96,2048]{1,0:T(8,128)(2,1)} async-done(((bf16[768,2048]{1,0:T(8,128)(2,1)}), bf16[96,2048]{1,0:T(8,128)(2,1)}) %reduce-scatter.42.cloned.1.call-update) | async-done | bytes 393232 | tf_op jit(solution)/shard_map/reduce_scatter | solution.py:372
  1721.5 73.9 %reduce-scatter.44.cloned.1.call-done = bf16[256,768]{1,0:T(8,128)(2,1)} async-done(((bf16[2048,768]{1,0:T(8,128)(2,1)}), bf16[256,768]{1,0:T(8,128)(2,1)}) %reduce-scatter.44.cloned.1.call-update) | async-done | bytes 393232 | tf_op jit(solution)/shard_map/reduce_scatter | solution.py:375
  1795.4 38.7 %reduce-scatter.30.cloned.1.call-done = bf16[96,768]{1,0:T(8,128)(2,1)} async-done(((bf16[768,768]{1,0:T(8,128)(2,1)}), bf16[96,768]{1,0:T(8,128)(2,1)}) %reduce-scatter.30.cloned.1.call-update) | async-done | bytes 147472 | tf_op jit(solution)/shard_map/reduce_scatter | solution.py:348
  1834.1 42.5 %reduce-scatter.32.cloned.1.call-done = bf16[96,768]{1,0:T(8,128)(2,1)} async-done(((bf16[768,768]{1,0:T(8,128)(2,1)}), bf16[96,768]{1,0:T(8,128)(2,1)}) %reduce-scatter.32.cloned.1.call-update) | async-done | bytes 147472 | tf_op jit(solution)/shard_map/reduce_scatter | solution.py:351
  1883.9 69.9 %all-reduce.3 = (f32[32,12]{0,1:T(8,128)}, f32[768]{0:T(1024)}, f32[768]{0:T(1024)}, f32[768]{0:T(1024)}) all-reduce(f32[32,12]{0,1:T(8,128)S(1)} %fusion.75, f32[768]{0:T(1024)S(1)} %get-tuple-element.775, f32[768]{0:T(1024)S(1)} %copy-done.78, f32[768]{0:T(1024)S(1)} %copy-done.79), channel_id=1, replica_groups=mesh['ctx'=16,'dp'=8] {'ctx','dp'}, use_global_device_ids=true, to_apply=%region_21.22 | all-reduce | flops 2688 | bytes 21504 | tf_op jit(solution)/shard_map/psum | solution.py:341
  1957.9 73.2 %all-reduce.7.cloned.1.call-done = (bf16[96,768]{0,1:T(8,128)(2,1)}, bf16[96,768]{0,1:T(8,128)(2,1)}, bf16[96,768]{1,0:T(8,128)(2,1)}, bf16[96,768]{1,0:T(8,128)...) async-done(((bf16[96,768]{0,1:T(8,128)(2,1)}, ...) | async-done | bytes 2359312 | tf_op jit(solution)/shard_map/psum | solution.py:385
  (554 shorter events, 835.2 us)
Async XLA Ops:
  10.0 247.3 %all-gather.16.cloned.1.call-start = ((), (), s32[]{:S(2)}) async-start(), calls=%async_computation.15 | async-start | bytes 1327104 | tf_op jit(solution)/shard_map/all_gather | solution.py:196
  10.6 264.8 %all-gather.20.cloned.1.call-start = ((), (), s32[]{:S(2)}) async-start(), calls=%async_computation.17 | async-start | bytes 3342336 | tf_op jit(solution)/shard_map/all_gather | solution.py:235
  51.4 276.5 %all-gather.24.cloned.1.call-start = ((), (), s32[]{:S(2)}) async-start(), calls=%async_computation.19 | async-start | bytes 3342336 | tf_op jit(solution)/shard_map/all_gather | solution.py:236
  93.2 269.5 %all-gather.26.cloned.1.call-start = ((), (), s32[]{:S(2)}) async-start(), calls=%async_computation.20 | async-start | bytes 1327104 | tf_op jit(solution)/shard_map/all_gather | solution.py:199
  94.0 310.7 %all-gather.28.cloned.1.call-start = ((), (), s32[]{:S(2)}) async-start(), calls=%async_computation.21 | async-start | bytes 1327104 | tf_op jit(solution)/shard_map/all_gather | solution.py:200
  94.7 369.4 %all-gather.32.cloned.1.call-start = ((), (), s32[]{:S(2)}) async-start(), calls=%async_computation.23 | async-start | bytes 3342336 | tf_op jit(solution)/shard_map/all_gather | solution.py:254
  135.0 381.6 %all-gather.36.cloned.1.call-start = ((), (), s32[]{:S(2)}) async-start(), calls=%async_computation.25 | async-start | bytes 3342336 | tf_op jit(solution)/shard_map/all_gather | solution.py:255
  176.7 375.4 %all-gather.38.cloned.1.call-start = ((), (), s32[]{:S(2)}) async-start(), calls=%async_computation.26 | async-start | bytes 1327104 | tf_op jit(solution)/shard_map/all_gather | solution.py:203
  177.3 451.2 %all-gather.40.cloned.1.call-start = ((), (), s32[]{:S(2)}) async-start(), calls=%async_computation.27 | async-start | bytes 3538944 | tf_op jit(solution)/shard_map/all_gather | solution.py:204
  178.1 523.0 %all-gather.42.cloned.1.call-start = ((), (), s32[]{:S(2)}) async-start(), calls=%async_computation.28 | async-start | bytes 3538944 | tf_op jit(solution)/shard_map/all_gather | solution.py:205
  178.6 595.0 %all-gather.44.cloned.1.call-start = ((), (), s32[]{:S(2)}) async-start(), calls=%async_computation.29 | async-start | bytes 3538944 | tf_op jit(solution)/shard_map/all_gather | solution.py:206
  179.2 1007.6 %reduce-scatter.50.cloned.1.call-start = ((), (), s32[]{:S(2)}) async-start(), calls=%async_computation.41 | async-start | bytes 3342336
  862.1 328.4 %reduce-scatter.52.cloned.1.call-start = ((), (), s32[]{:S(2)}) async-start(), calls=%async_computation.42 | async-start | bytes 3342336
  889.4 350.0 %reduce-scatter.46.cloned.1.call-start = ((), (), s32[]{:S(2)}) async-start(), calls=%async_computation.39 | async-start | bytes 3342336
  1194.2 247.6 %reduce-scatter.28.cloned.1.call-start = ((), (), s32[]{:S(2)}) async-start(), calls=%async_computation.30 | async-start | bytes 1327104 | tf_op jit(solution)/shard_map/reduce_scatter | solution.py:345
  1196.0 288.4 %reduce-scatter.34.cloned.1.call-start = ((), (), s32[]{:S(2)}) async-start(), calls=%async_computation.33 | async-start | bytes 1327104 | tf_op jit(solution)/shard_map/reduce_scatter | solution.py:354
  1197.6 329.4 %reduce-scatter.36.cloned.1.call-start = ((), (), s32[]{:S(2)}) async-start(), calls=%async_computation.34 | async-start | bytes 1327104 | tf_op jit(solution)/shard_map/reduce_scatter | solution.py:357
  1199.3 370.6 %reduce-scatter.38.cloned.1.call-start = ((), (), s32[]{:S(2)}) async-start(), calls=%async_computation.35 | async-start | bytes 1327104 | tf_op jit(solution)/shard_map/reduce_scatter | solution.py:366
  1200.9 446.8 %reduce-scatter.40.cloned.1.call-start = ((), (), s32[]{:S(2)}) async-start(), calls=%async_computation.36 | async-start | bytes 3538944 | tf_op jit(solution)/shard_map/reduce_scatter | solution.py:369
  1203.8 517.7 %reduce-scatter.42.cloned.1.call-start = ((), (), s32[]{:S(2)}) async-start(), calls=%async_computation.37 | async-start | bytes 3538944 | tf_op jit(solution)/shard_map/reduce_scatter | solution.py:372
  1206.6 588.7 %reduce-scatter.44.cloned.1.call-start = ((), (), s32[]{:S(2)}) async-start(), calls=%async_computation.38 | async-start | bytes 3538944 | tf_op jit(solution)/shard_map/reduce_scatter | solution.py:375
  1209.4 624.7 %reduce-scatter.30.cloned.1.call-start = ((), (), s32[]{:S(2)}) async-start(), calls=%async_computation.31 | async-start | bytes 1327104 | tf_op jit(solution)/shard_map/reduce_scatter | solution.py:348
  1242.6 633.9 %reduce-scatter.32.cloned.1.call-start = ((), (), s32[]{:S(2)}) async-start(), calls=%async_computation.32 | async-start | bytes 1327104 | tf_op jit(solution)/shard_map/reduce_scatter | solution.py:351
  1322.7 708.4 %all-reduce.7.cloned.1.call-start = ((), (), s32[]{:S(2)}) async-start(), calls=%async_computation.45 | async-start | bytes 4915200 | tf_op jit(solution)/shard_map/psum | solution.py:385
  (130 other events, 5846.1 us)
Sparse Core Ops, SparseCore 0:
  50.5 40.1 all-gather.21
  175.8 40.1 all-gather.15
  218.7 56.6 all-gather.19
  278.3 49.6 all-gather.23
  364.4 40.2 all-gather.27
  407.4 56.6 all-gather.31
  466.9 49.6 all-gather.35
  553.8 74.6 all-gather.39
  630.0 71.0 all-gather.41
  702.6 71.0 all-gather.43
  862.2 74.1 reduce-scatter.49
  940.3 74.2 reduce-scatter.51
  1165.0 74.3 reduce-scatter.45
  1243.4 74.2 reduce-scatter.47
  1358.7 40.2 reduce-scatter.55
  1401.4 40.2 reduce-scatter.27
  1444.1 40.2 reduce-scatter.33
  1486.7 40.2 reduce-scatter.35
  1529.4 40.4 reduce-scatter.37
  1572.2 75.4 reduce-scatter.39
  1650.0 71.4 reduce-scatter.41
  1723.9 71.4 reduce-scatter.43
  1836.3 40.1 reduce-scatter.31
  1880.6 150.4 all-reduce.6
  (7 shorter events, 258.8 us)
where the time goes:
time: 2060 us; the launch traced here: 2050 us
  waiting for transfers between devices  1350 us (66%)
  local copies, waits for them, and re-layouts  388 us (19%)
  matrix products  183 us (9%)
  blocking collectives  69.9 us (3%)
  other arithmetic  48.8 us (2%)
    unnamed x37, waiting for transfers between devices  186 us
    unnamed x190, local copies, waits for them, and re-layouts  120 us
    reduce_scatter x1, waiting for transfers between devices, body(): lax.psum_scatter(grad_gate_w.astype(jnp.bfloat16), 'dp', scatter_dimensio...  77.8 us
    reduce_scatter x1, waiting for transfers between devices, body(): lax.psum_scatter(grad_down.astype(jnp.bfloat16), 'dp', scatter_dimension=...  73.9 us
    all_gather x1, waiting for transfers between devices, body(): lax.all_gather(gate_weight, 'dp', axis=0, tiled=True)  73.8 us
    reduce_scatter x1, waiting for transfers between devices, body(): lax.psum_scatter(grad_up_w.astype(jnp.bfloat16), 'dp', scatter_dimension=...  73.7 us
    psum x1, waiting for transfers between devices, body(): lax.psum(pieces[5].astype(jnp.bfloat16), 'ctx').astype(jnp.float32)  73.2 us
    psum x1, blocking collectives, body(): lax.psum((grad_gain_one, grad_gain_two, grad_gain_three, local_table), ('...  69.9 us
  transfers between devices with their start and end apart: 31, of which 28 were waited for; matrix products, arithmetic and copies ran while one was open for 24% of the time, Pallas kernels for 0%

commit v1 on v0

--- a/solution.py
+++ b/solution.py
@@ -1,10 +1,494 @@
+import functools
 import math
-
 import jax
 import jax.numpy as jnp
 from jax import lax
+from jax.experimental import pallas as pl
+from jax.experimental.pallas import tpu as pltpu
 from jax.sharding import PartitionSpec as P
 
+MESH = pl.DeviceIdType.MESH
+ANY = pl.BlockSpec(memory_space=pl.ANY)
+VMEM = pl.BlockSpec(memory_space=pltpu.VMEM)
+
+
+class Place:
+    def __init__(self):
+        c = lax.axis_index("ctx")
+        d = lax.axis_index("dp")
+        self.c, self.d = c, d
+        self.x_hi = c // 8
+        self.z = (c // 2) % 4
+        self.core = c % 2
+        self.y = d // 2
+        self.x_lo = d % 2
+        self.y_a = self.y + 1 - 2 * (self.y % 2)
+        self.y_b = 3 - self.y
+        self.y_ab = 3 - self.y_a
+        self.z_a = self.z + 1 - 2 * (self.z % 2)
+        self.z_b = 3 - self.z
+        self.z_ab = 3 - self.z_a
+        far_lo, far_hi = 1 - self.x_lo, 1 - self.x_hi
+        self.x = self.x_lo * 2 + self.x_hi
+        self.x_a = far_lo * 2 + self.x_hi
+        self.x_b = far_lo * 2 + far_hi
+        self.x_ab = self.x_lo * 2 + far_hi
+        same = self.x_hi * 8 + self.z * 2 + self.core
+        self.dev = {
+            "core": (self.x_hi * 8 + self.z * 2 + 1 - self.core, d),
+            "ya": (same, self.y_a * 2 + self.x_lo),
+            "yb": (same, self.y_b * 2 + self.x_lo),
+            "za": (self.x_hi * 8 + self.z_a * 2 + self.core, d),
+            "zb": (self.x_hi * 8 + self.z_b * 2 + self.core, d),
+            "xa": (same, self.y * 2 + far_lo),
+            "xb": (far_hi * 8 + self.z * 2 + self.core, self.y * 2 + far_lo),
+            "xab": (far_hi * 8 + self.z * 2 + self.core, d),
+        }
+
+    def greet(self, names):
+        barrier = pltpu.get_barrier_semaphore()
+        for name in names:
+            pl.semaphore_signal(
+                barrier, inc=1, device_id=self.dev[name], device_id_type=MESH
+            )
+        pl.semaphore_wait(barrier, len(names))
+
+    def send(self, name, src, dst, send_sem, recv_sem):
+        copy = pltpu.make_async_remote_copy(
+            src_ref=src,
+            dst_ref=dst,
+            send_sem=send_sem,
+            recv_sem=recv_sem,
+            device_id=self.dev[name],
+            device_id_type=MESH,
+        )
+        copy.start()
+        return copy
+
+
+GATHER_PLAN = (
+    ((0, "pair", 0), (8, "za", 0), (9, "zb", 0)),
+    ((1, "pair", 0), (8, "za", 1), (9, "zb", 1)),
+    ((2, "pair", 0), (3, "za", 0), (10, "zb", 0)),
+    ((5, "pair", 0), (4, "za", 0), (10, "zb", 1)),
+    ((6, "pair", 0), (7, "za", 0), (10, "zb", 2)),
+)
+
+
+class Chain:
+    def __init__(self, me, source, target, kind, half, piece, pieces, sems):
+        rows, cols = source.shape
+        width = cols // 2 // pieces
+        self.me, self.source, self.target, self.kind = me, source, target, kind
+        self.sems, self.slot, self.copies = sems, 0, []
+        self.all_rows = pl.ds(0, rows)
+        if kind == "pair":
+            self.rows = pl.ds(half * (rows // 2), rows // 2)
+            self.all_rows = self.rows
+            flip = half == 1
+        else:
+            bit = me.z % 2 if kind == "za" else me.z // 2
+            self.rows = pl.ds(pl.multiple_of(bit * (rows // 2), 16), rows // 2)
+            flip = kind == "zb"
+        self.cols = pl.ds(pl.multiple_of(me.core * (cols // 2) + piece * width, 128), width)
+        self.other = pl.ds(pl.multiple_of((1 - me.core) * (cols // 2) + piece * width, 128), width)
+        self.first, self.second = ("yb", "ya") if flip else ("ya", "yb")
+        self.near = me.y_b if flip else me.y_a
+        self.side = "xb" if flip else "xa"
+        self.stages = 4 if kind == "pair" else 5
+
+    def go(self, name, src, dst):
+        send_sem, recv_sem, index = self.sems
+        copy = self.me.send(
+            name, src, dst, send_sem.at[index, self.slot], recv_sem.at[index, self.slot]
+        )
+        self.slot += 1
+        self.copies.append(copy)
+        return copy
+
+    def run(self, stage):
+        me, out = self.me, self.target
+        if stage == 0:
+            mine = self.source.at[self.rows, self.cols]
+            spot = out.at[me.y, me.x_lo, self.rows, self.cols]
+            self.first_copy = self.go(self.first, mine, spot)
+            self.second_copy = self.go(self.second, mine, spot)
+            self.own_copy = self.go(
+                "core",
+                self.source.at[self.rows, self.other],
+                out.at[me.y, me.x_lo, self.rows, self.other],
+            )
+        elif stage == 1:
+            self.first_copy.wait_recv()
+            got = out.at[self.near, me.x_lo, self.rows, self.cols]
+            self.third_copy = self.go(self.second, got, got)
+        elif stage == 2:
+            self.second_copy.wait_recv()
+            self.own_copy.wait_recv()
+            self.third_copy.wait_recv()
+            got = out.at[:, me.x_lo, self.rows, self.cols]
+            self.last = self.go(self.side, got, got)
+        elif stage == 3 and self.kind != "pair":
+            self.last.wait_recv()
+            got = out.at[:, :, self.rows, self.cols]
+            self.last = self.go(self.kind, got, got)
+        elif stage == self.stages - 1:
+            self.last.wait_recv()
+            got = out.at[:, :, self.all_rows, self.cols]
+            self.last = self.go("core", got, got)
+        elif stage == self.stages:
+            self.last.wait_recv()
+
+
+def gather_kernel(count, plan, *refs):
+    ins, outs = refs[:count], refs[count : 2 * count]
+    send_sem, recv_sem = refs[2 * count :]
+    me = Place()
+    me.greet(("ya", "yb", "xa", "xb", "za", "zb", "core"))
+    pieces = {}
+    for group in plan:
+        for array, kind, piece in group:
+            pieces[array] = max(pieces.get(array, 0), piece + 1)
+    groups = []
+    index = 0
+    for group in plan:
+        chains = []
+        for array, kind, piece in group:
+            for half in range(2 if kind == "pair" else 1):
+                chains.append(
+                    Chain(
+                        me, ins[array], outs[array], kind, half, piece, pieces[array],
+                        (send_sem, recv_sem, index),
+                    )
+                )
+                index += 1
+        groups.append(chains)
+    for chain in groups[0]:
+        chain.run(0)
+    for tick in range(1, len(groups) + 6):
+        for stage in (5, 4, 3, 2, 1, 0):
+            spot = tick - stage
+            if stage == 0 and tick < len(groups):
+                for chain in groups[tick]:
+                    chain.run(0)
+            elif stage > 0 and 0 <= spot < len(groups):
+                for chain in groups[spot]:
+                    chain.run(stage)
+    for chains in groups:
+        for chain in chains:
+            for copy in chain.copies:
+                copy.wait_send()
+
+
+def gather_weights(shards, plan, collective_id):
+    count = len(shards)
+    chains = sum(2 if kind == "pair" else 1 for group in plan for _, kind, _ in group)
+    outs = pl.pallas_call(
+        functools.partial(gather_kernel, count, plan),
+        out_shape=[
+            jax.ShapeDtypeStruct((4, 2) + shard.shape, shard.dtype) for shard in shards
+        ],
+        in_specs=[ANY] * count,
+        out_specs=[ANY] * count,
+        scratch_shapes=[
+            pltpu.SemaphoreType.DMA((chains, 7)),
+            pltpu.SemaphoreType.DMA((chains, 7)),
+        ],
+        compiler_params=pltpu.CompilerParams(collective_id=collective_id, has_side_effects=True),
+        name="gather_weights",
+    )(*shards)
+    return [out.reshape(8 * out.shape[2], out.shape[3]) for out in outs]
+
+AXES = ("y", "x", "z")
+
+
+def reduce_kernel(
+    grads, small, *refs
+):
+    outs, small_out = refs[:11], refs[11]
+    (acc, r0, r1, r2, r3, r4, r5, r6, full, sm_in,
+     load_sem, send_sem, recv_sem, sm_send, sm_recv, ag_send, ag_recv) = refs[12:]
+    recvs = (r1, r2, r3, r4, r5, r6)
+    me = Place()
+    me.greet(("core", "ya", "yb", "xa", "xb", "za", "zb", "xab"))
+    spots = {
+        "y": (me.y, me.y_a, me.y_b, me.y_ab),
+        "x": (me.x, me.x_a, me.x_b, me.x_ab),
+        "z": (me.z, me.z_a, me.z_b, me.z_ab),
+    }
+    parts = range(6)
+    started = []
+
+    def go(name, src, dst, send, recv):
+        copy = me.send(name, src, dst, send, recv)
+        started.append(copy)
+        return copy
+
+    small_out[...] = small[...]
+    small_steps = ("core", "ya", "yb", "xa", "xb", "za", "zb")
+    small_copies = []
+
+    def small_start(step):
+        small_copies.append(
+            me.send(small_steps[step], small_out, sm_in.at[step], sm_send.at[step], sm_recv.at[step])
+        )
+
+    def small_end(step):
+        small_copies[step].wait()
+        small_out[...] = small_out[...] + sm_in[step]
+
+    small_start(0)
+
+    def order(part):
+        first = (part // 2) % 3
+        return [AXES[(first + k) % 3] for k in range(3)]
+
+    def region(part, picks):
+        return (part,) + tuple(picks.get(axis, slice(None)) for axis in AXES)
+
+    def at(ref, index):
+        return ref.at[index]
+
+    core_copies, loads = [], []
+    for part in parts:
+        core_copies.append(
+            go("core", grads.at[1 - me.core, part], r0.at[part], send_sem.at[part, 0], recv_sem.at[part, 0])
+        )
+        load = pltpu.make_async_copy(grads.at[me.core, part], acc.at[part], load_sem.at[part])
+        load.start()
+        loads.append(load)
+
+    def add(index, source, source_index):
+        acc[index] = acc[index] + source[source_index]
+
+    def dims(part):
+        return ("a", "b") if part % 2 == 0 else ("b", "a")
+
+    def add_first(part, picks):
+        axis = order(part)[0]
+        rest = [name for name in AXES if name != axis]
+
+        def step(k, carry):
+            index = region(part, {**picks, rest[0]: k})
+            acc[index] = acc[index] + r0[index]
+            return carry
+
+        lax.fori_loop(0, 4, step, 0)
+
+    pending = {}
+    for part in parts:
+        axis = order(part)[0]
+        me_at, a_at, b_at, ab_at = spots[axis]
+        first, second = dims(part)
+        sent = (a_at, ab_at) if first == "a" else (b_at, ab_at)
+        core_copies[part].wait_recv()
+        loads[part].wait()
+        pending[part] = []
+        for slot, spot in enumerate(sent):
+            add_first(part, {axis: spot})
+            pending[part].append(
+                go(
+                    axis + first,
+                    at(acc, region(part, {axis: spot})),
+                    r1.at[part, slot],
+                    send_sem.at[part, 1 + slot],
+                    recv_sem.at[part, 1 + slot],
+                )
+            )
+    small_end(0)
+    small_start(1)
+    for part in parts:
+        axis = order(part)[0]
+        me_at, a_at, b_at, ab_at = spots[axis]
+        first, second = dims(part)
+        kept = b_at if first == "a" else a_at
+        add_first(part, {axis: kept})
+        add_first(part, {axis: me_at})
+
+    sem_at = {part: 3 for part in parts}
+
+    def next_sem(part):
+        sem_at[part] += 1
+        return send_sem.at[part, sem_at[part] - 1], recv_sem.at[part, sem_at[part] - 1]
+
+    for level in range(3):
+        one, two = recvs[2 * level], recvs[2 * level + 1]
+        for part in parts:
+            axes = order(part)
+            axis = axes[level]
+            first, second = dims(part)
+            me_at, a_at, b_at, ab_at = spots[axis]
+            kept = b_at if first == "a" else a_at
+            fixed = {name: spots[name][0] for name in axes[:level]}
+            for copy in pending[part]:
+                copy.wait_recv()
+            add(region(part, {**fixed, axis: kept}), one, (part, 1))
+            send, recv = next_sem(part)
+            pending[part] = [
+                go(axis + second, at(acc, region(part, {**fixed, axis: kept})), two.at[part], send, recv)
+            ]
+        for part in parts:
+            axes = order(part)
+            fixed = {name: spots[name][0] for name in axes[: level + 1]}
+            add(region(part, fixed), one, (part, 0))
+        small_end(2 * level + 1)
+        small_start(2 * level + 2)
+        for part in parts:
+            axes = order(part)
+            fixed = {name: spots[name][0] for name in axes[: level + 1]}
+            for copy in pending[part]:
+                copy.wait_recv()
+            add(region(part, fixed), two, (part,))
+            if level == 2:
+                continue
+            axis = axes[level + 1]
+            first, second = dims(part)
+            me_at, a_at, b_at, ab_at = spots[axis]
+            sent = (a_at, ab_at) if first == "a" else (b_at, ab_at)
+            pending[part] = []
+            for slot, spot in enumerate(sent):
+                send, recv = next_sem(part)
+                pending[part].append(
+                    go(
+                        axis + first,
+                        at(acc, region(part, {**fixed, axis: spot})),
+                        recvs[2 * level + 2].at[part, slot],
+                        send,
+                        recv,
+                    )
+                )
+        small_end(2 * level + 2)
+        if level < 2:
+            small_start(2 * level + 3)
+
+    here = me.x_hi * 4 + me.z
+    there = (1 - me.x_hi) * 4 + me.z
+    for part in parts:
+        full[here, me.core, part] = acc[part, me.y, me.x, me.z]
+    used = [0]
+
+    def pass_on(name, group, half):
+        index = used[0]
+        used[0] += 1
+        src = full.at[group, me.core, pl.ds(3 * half, 3)]
+        return go(name, src, src, ag_send.at[index], ag_recv.at[index])
+
+    early = [pass_on("xab", here, half) for half in range(2)]
+    near = [pass_on("za", here, 0), pass_on("zb", here, 1)]
+    far = []
+    for half in range(2):
+        early[half].wait_recv()
+        far.append(pass_on(("za", "zb")[half], there, half))
+    base, base_far = me.x_hi * 4, (1 - me.x_hi) * 4
+    ends = [pass_on("zb", here, 0), pass_on("za", here, 1)]
+    ends += [pass_on("zb", there, 0), pass_on("za", there, 1)]
+    for half in range(2):
+        got = (me.z_a, me.z_b)[half]
+        near[half].wait_recv()
+        ends.append(pass_on(("zb", "za")[half], base + got, half))
+    for half in range(2):
+        got = (me.z_a, me.z_b)[half]
+        far[half].wait_recv()
+        ends.append(pass_on(("zb", "za")[half], base_far + got, half))
+    for copy in ends:
+        copy.wait_recv()
+    last = go("core", full.at[:, me.core], full.at[:, me.core], ag_send.at[used[0]], ag_recv.at[used[0]])
+
+    def place(o):
+        group, core = o // 2, o % 2
+        for part in parts:
+            rows = pl.ds(16 * part, 16)
+            outs[group][rows, pl.ds(core * 384, 384)] = full[group, core, part, :, 0:384]
+            outs[8][rows, pl.ds(128 * o, 128)] = full[group, core, part, :, 384:512]
+            outs[9][rows, pl.ds(128 * o, 128)] = full[group, core, part, :, 512:640]
+            outs[10][pl.ds(16 * o, 16), pl.ds(128 * part, 128)] = full[group, core, part, :, 640:768]
+
+    last.wait_recv()
+    for o in range(16):
+        place(o)
+    for copy in started:
+        copy.wait_send()
+
+
+def reduce_weights(grads, small, collective_id):
+    bf = jnp.bfloat16
+    shapes = [(96, 768)] * 8 + [(96, 2048)] * 2 + [(256, 768)]
+    return pl.pallas_call(
+        reduce_kernel,
+        out_shape=[jax.ShapeDtypeStruct(shape, bf) for shape in shapes]
+        + [jax.ShapeDtypeStruct(small.shape, small.dtype)],
+        in_specs=[ANY, VMEM],
+        out_specs=[VMEM] * 12,
+        scratch_shapes=[
+            pltpu.VMEM((6, 4, 4, 4, 16, 768), bf),
+            pltpu.VMEM((6, 4, 4, 4, 16, 768), bf),
+            pltpu.VMEM((6, 2, 4, 4, 16, 768), bf),
+            pltpu.VMEM((6, 4, 4, 16, 768), bf),
+            pltpu.VMEM((6, 2, 4, 16, 768), bf),
+            pltpu.VMEM((6, 4, 16, 768), bf),
+            pltpu.VMEM((6, 2, 16, 768), bf),
+            pltpu.VMEM((6, 16, 768), bf),
+            pltpu.VMEM((8, 2, 6, 16, 768), bf),
+            pltpu.VMEM((7,) + small.shape, small.dtype),
+            pltpu.SemaphoreType.DMA((6,)),
+            pltpu.SemaphoreType.DMA((6, 10)),
+            pltpu.SemaphoreType.DMA((6, 10)),
+            pltpu.SemaphoreType.DMA((7,)),
+            pltpu.SemaphoreType.DMA((7,)),
+            pltpu.SemaphoreType.DMA((16,)),
+            pltpu.SemaphoreType.DMA((16,)),
+        ],
+        compiler_params=pltpu.CompilerParams(
+            collective_id=collective_id, has_side_effects=True, vmem_limit_bytes=56 * 2**20
+        ),
+        name="reduce_weights",
+    )(grads, small)
+
+
+def outer_kernel(acts, grads, third, gate, up, mixed, cot, out):
+    def transposed_dot(left, right):
+        return lax.dot_general(
+            left, right, (((0,), (0,)), ((), ())), preferred_element_type=jnp.float32
+        ).astype(jnp.bfloat16)
+
+    attn = transposed_dot(acts[0], grads[0])
+    wide = transposed_dot(third[...], jnp.concatenate([gate[...], up[...]], axis=1))
+    down = transposed_dot(mixed[0], cot[...])
+    for row in range(8):
+        for part in range(6):
+            begin = row * 96 + part * 16
+            where = (0, part, row // 2, row % 2, 0, 0)
+            out[where + (slice(None), slice(0, 384))] = attn[begin : begin + 16]
+            out[where + (slice(None), slice(384, 640))] = wide[begin : begin + 16]
+            out[where + (slice(None), slice(640, 768))] = down[
+                row * 16 : row * 16 + 16, part * 128 : part * 128 + 128
+            ]
+
+
+def outer_products(acts, grads, third, gate, up, mixed, cot):
+    tokens = third.shape[0]
+    mixed_cut = mixed.reshape(tokens, 8, 16, 16).transpose(2, 0, 1, 3).reshape(16, tokens, 128)
+    out = pl.pallas_call(
+        outer_kernel,
+        grid=(16,),
+        out_shape=jax.ShapeDtypeStruct((2, 6, 4, 2, 2, 4, 16, 768), jnp.bfloat16),
+        in_specs=[
+            pl.BlockSpec((1, tokens, 768), lambda o: (o // 2, 0, 0)),
+            pl.BlockSpec((1, tokens, 384), lambda o: (o // 2, 0, o % 2)),
+            pl.BlockSpec((tokens, 768), lambda o: (0, 0)),
+            pl.BlockSpec((tokens, 128), lambda o: (0, o)),
+            pl.BlockSpec((tokens, 128), lambda o: (0, o)),
+            pl.BlockSpec((1, tokens, 128), lambda o: (o, 0, 0)),
+            pl.BlockSpec((tokens, 768), lambda o: (0, 0)),
+        ],
+        out_specs=pl.BlockSpec(
+            (1, 6, 4, 2, 1, 1, 16, 768),
+            lambda o: (o % 2, 0, 0, 0, o // 8, (o // 2) % 4, 0, 0),
+        ),
+        compiler_params=pltpu.CompilerParams(vmem_limit_bytes=32 * 2**20),
+        name="outer_products",
+    )(acts, grads, third, gate, up, mixed_cut, cot)
+    return out.reshape(2, 6, 4, 4, 4, 16, 768)
 EPSILON = 1e-06
 NEGATIVE = -1e30
 PRECISE = lax.Precision.HIGHEST
@@ -192,18 +676,14 @@
     bucket_count = bias_table.shape[0]
     seq_count, row_count, model_width = layer_input.shape
     head_size = model_width // head_count
-    weights = (
-        lax.all_gather(self_query, "dp", axis=0, tiled=True),
-        lax.all_gather(self_key, "dp", axis=0, tiled=True),
-        lax.all_gather(self_value, "dp", axis=0, tiled=True),
-        lax.all_gather(self_output, "dp", axis=0, tiled=True),
-        lax.all_gather(cross_query, "dp", axis=0, tiled=True),
-        lax.all_gather(cross_key, "dp", axis=0, tiled=True),
-        lax.all_gather(cross_value, "dp", axis=0, tiled=True),
-        lax.all_gather(cross_output, "dp", axis=0, tiled=True),
-        lax.all_gather(gate_weight, "dp", axis=0, tiled=True),
-        lax.all_gather(up_weight, "dp", axis=0, tiled=True),
-        lax.all_gather(down_weight, "dp", axis=0, tiled=True),
+    weights = gather_weights(
+        (
+            self_query, self_key, self_value, self_output,
+            cross_query, cross_key, cross_value, cross_output,
+            gate_weight, up_weight, down_weight,
+        ),
+        GATHER_PLAN,
+        0,
     )
     position = lax.axis_index("ctx")
     query_begin = position * row_count
@@ -267,18 +747,14 @@
     mixed_low = mixed_act.astype(jnp.bfloat16)
     final = after_cross + project(mixed_low, weights[10])
     layer_output = final.astype(jnp.bfloat16)
-    grad_down = outer_sum(mixed_low, cotangent)
     grad_gate, grad_up = back_mix(project_back(cotangent, weights[10]))
     grad_gate = grad_gate.astype(jnp.bfloat16)
     grad_up = grad_up.astype(jnp.bfloat16)
-    grad_gate_w = outer_sum(normed_three, grad_gate)
-    grad_up_w = outer_sum(normed_three, grad_up)
     grad_normed = project_back(grad_gate, weights[8]) + project_back(grad_up, weights[9])
     grad_back, grad_gain_three = back_third(grad_normed)
     grad_after = cotangent.astype(jnp.float32) + grad_back
-    branch_grad = grad_after.astype(jnp.bfloat16)
-    grad_cout = outer_sum(crossed, branch_grad)
-    grad_crossed = project_back(branch_grad, weights[7]).astype(jnp.bfloat16)
+    branch_after = grad_after.astype(jnp.bfloat16)
+    grad_crossed = project_back(branch_after, weights[7]).astype(jnp.bfloat16)
     grad_cross_heads = split_heads(grad_crossed, head_count)
     cross_all = (
         lax.all_gather(cross_pair[0], "ctx", axis=1, tiled=True),
@@ -298,14 +774,10 @@
     grad_cquery = join_heads(cross_back[0]).astype(jnp.bfloat16)
     grad_ckeys = join_heads(cross_kv_sum[0]).astype(jnp.bfloat16)
     grad_cvalues = join_heads(cross_kv_sum[1]).astype(jnp.bfloat16)
-    grad_cq_w = outer_sum(normed_two, grad_cquery)
-    grad_ck_w = outer_sum(encoder_states, grad_ckeys)
-    grad_cv_w = outer_sum(encoder_states, grad_cvalues)
     grad_encoder = project_back(grad_ckeys, weights[5]) + project_back(grad_cvalues, weights[6])
     grad_back, grad_gain_two = back_second(project_back(grad_cquery, weights[4]))
     grad_middle = grad_after + grad_back
     branch_grad = grad_middle.astype(jnp.bfloat16)
-    grad_sout = outer_sum(attended, branch_grad)
     grad_attended = project_back(branch_grad, weights[3]).astype(jnp.bfloat16)
     grad_self_heads = split_heads(grad_attended, head_count)
     self_all = (
@@ -326,9 +798,6 @@
     grad_queries = join_heads(self_back[0]).astype(jnp.bfloat16)
     grad_keys = join_heads(self_kv_sum[0]).astype(jnp.bfloat16)
     grad_values = join_heads(self_kv_sum[1]).astype(jnp.bfloat16)
-    grad_sq_w = outer_sum(normed_one, grad_queries)
-    grad_sk_w = outer_sum(normed_one, grad_keys)
-    grad_sv_w = outer_sum(normed_one, grad_values)
     grad_normed = (
         project_back(grad_queries, weights[0])
         + project_back(grad_keys, weights[1])
@@ -338,77 +807,35 @@
     grad_input = grad_middle + grad_back
     offset_grads = self_back[3][:, margin : margin + distance_count]
     local_table = jnp.transpose(jnp.dot(offset_grads, table_hot, precision=PRECISE))
-    small_sums = lax.psum(
-        (grad_gain_one, grad_gain_two, grad_gain_three, local_table), ("ctx", "dp")
-    )
-    pieces = (
-        lax.psum_scatter(
-            grad_sq_w.astype(jnp.bfloat16), "dp", scatter_dimension=0, tiled=True
-        ).astype(jnp.float32),
-        lax.psum_scatter(
-            grad_sk_w.astype(jnp.bfloat16), "dp", scatter_dimension=0, tiled=True
-        ).astype(jnp.float32),
-        lax.psum_scatter(
-            grad_sv_w.astype(jnp.bfloat16), "dp", scatter_dimension=0, tiled=True
-        ).astype(jnp.float32),
-        lax.psum_scatter(
-            grad_sout.astype(jnp.bfloat16), "dp", scatter_dimension=0, tiled=True
-        ).astype(jnp.float32),
-        lax.psum_scatter(
-            grad_cq_w.astype(jnp.bfloat16), "dp", scatter_dimension=0, tiled=True
-        ).astype(jnp.float32),
-        lax.psum_scatter(
-            grad_ck_w.astype(jnp.bfloat16), "dp", scatter_dimension=0, tiled=True
-        ).astype(jnp.float32),
-        lax.psum_scatter(
-            grad_cv_w.astype(jnp.bfloat16), "dp", scatter_dimension=0, tiled=True
-        ).astype(jnp.float32),
-        lax.psum_scatter(
-            grad_cout.astype(jnp.bfloat16), "dp", scatter_dimension=0, tiled=True
-        ).astype(jnp.float32),
-        lax.psum_scatter(
-            grad_gate_w.astype(jnp.bfloat16), "dp", scatter_dimension=0, tiled=True
-        ).astype(jnp.float32),
-        lax.psum_scatter(
-            grad_up_w.astype(jnp.bfloat16), "dp", scatter_dimension=0, tiled=True
-        ).astype(jnp.float32),
-        lax.psum_scatter(
-            grad_down.astype(jnp.bfloat16), "dp", scatter_dimension=0, tiled=True
-        ).astype(jnp.float32),
-    )
-    shards = (
-        lax.psum(pieces[0].astype(jnp.bfloat16), "ctx").astype(jnp.float32),
-        lax.psum(pieces[1].astype(jnp.bfloat16), "ctx").astype(jnp.float32),
-        lax.psum(pieces[2].astype(jnp.bfloat16), "ctx").astype(jnp.float32),
-        lax.psum(pieces[3].astype(jnp.bfloat16), "ctx").astype(jnp.float32),
-        lax.psum(pieces[4].astype(jnp.bfloat16), "ctx").astype(jnp.float32),
-        lax.psum(pieces[5].astype(jnp.bfloat16), "ctx").astype(jnp.float32),
-        lax.psum(pieces[6].astype(jnp.bfloat16), "ctx").astype(jnp.float32),
-        lax.psum(pieces[7].astype(jnp.bfloat16), "ctx").astype(jnp.float32),
-        lax.psum(pieces[8].astype(jnp.bfloat16), "ctx").astype(jnp.float32),
-        lax.psum(pieces[9].astype(jnp.bfloat16), "ctx").astype(jnp.float32),
-        lax.psum(pieces[10].astype(jnp.bfloat16), "ctx").astype(jnp.float32),
-    )
+    small = jnp.concatenate(
+        [grad_gain_one, grad_gain_two, grad_gain_three, local_table.reshape(-1)]
+    )
+    small = jnp.pad(small, (0, 24 * 128 - small.shape[0])).reshape(24, 128)
+    partials = outer_products(
+        jnp.concatenate(
+            [normed_one, normed_one, normed_one, attended, normed_two, encoder_states, encoder_states, crossed]
+        ),
+        jnp.concatenate(
+            [grad_queries, grad_keys, grad_values, branch_grad, grad_cquery, grad_ckeys, grad_cvalues, branch_after]
+        ),
+        normed_three[0],
+        grad_gate[0],
+        grad_up[0],
+        mixed_low[0],
+        cotangent[0],
+    )
+    *shards, sums = reduce_weights(partials, small, 1)
+    sums = sums.reshape(-1)
+    width = model_width
     return (
         layer_output,
         grad_input,
         grad_encoder,
-        small_sums[3],
-        small_sums[0],
-        small_sums[1],
-        small_sums[2],
-        shards[0],
-        shards[1],
-        shards[2],
-        shards[3],
-        shards[4],
-        shards[5],
-        shards[6],
-        shards[7],
-        shards[8],
-        shards[9],
-        shards[10],
-    )
+        sums[3 * width : 3 * width + bucket_count * head_count].reshape(bucket_count, head_count),
+        sums[:width],
+        sums[width : 2 * width],
+        sums[2 * width : 3 * width],
+    ) + tuple(shard.astype(jnp.float32) for shard in shards)
 
 
 def solution(mesh):

time: 2060 us -> 1100 us (0.53)
  waiting for transfers between devices: 1350 us -> 304 us
  Pallas kernels: 0 us -> 168 us
  blocking collectives: 69.9 us -> 0 us
  matrix products: 183 us -> 149 us
    reduce_scatter x9 -> x0, waiting for transfers between devices: 476 us -> none  [the longest x1 77.8 us: body(): lax.psum_scatter(grad_gate_w.astype(jnp.bfloat16), 'dp', scatter_dimensio...]
    all_gather x11 -> x0, waiting for transfers between devices: 458 us -> none  [the longest x1 73.8 us: body(): lax.all_gather(gate_weight, 'dp', axis=0, tiled=True)]
    pallas_call x0 -> x3, Pallas kernels: none -> 168 us  [the longest x1 84.8 us: reduce_weights(): pl.pallas_call(reduce_kernel, out_shape=[jax.ShapeDtypeStruct(shape, bf)...]
    psum x1 -> x0, waiting for transfers between devices: 73.2 us -> none  [body(): lax.psum(pieces[5].astype(jnp.bfloat16), 'ctx').astype(jnp.float32)]
    psum x1 -> x0, blocking collectives: 69.9 us -> none  [body(): lax.psum((grad_gain_one, grad_gain_two, grad_gain_three, local_table), ('...]
    all_gather x1, waiting for transfers between devices: 37 us -> 2.48 us  [body(): lax.all_gather(self_pair[1], 'ctx', axis=1, tiled=True)]
    unnamed x37 -> x12, waiting for transfers between devices: 186 us -> 215 us
    unnamed x190 -> x184, local copies, waits for them, and re-layouts: 120 us -> 114 us
  transfers between devices with their start and end apart: 31 -> 8, of which waited for: 28 -> 6; matrix products, arithmetic and copies ran while one was open for 24% -> 18% of each run, Pallas kernels for 0% -> 0%
where the time goes in v1:
time: 1100 us; the launch traced here: 1090 us
  local copies, waits for them, and re-layouts  395 us (36%)
  waiting for transfers between devices  304 us (28%)
  Pallas kernels  168 us (15%)
  matrix products  149 us (14%)
  other arithmetic  58.9 us (5%)
  between operations  15.7 us (1%)
    unnamed x12, waiting for transfers between devices  215 us
    unnamed x184, local copies, waits for them, and re-layouts  114 us
    pallas_call x1, Pallas kernels, reduce_weights(): pl.pallas_call(reduce_kernel, out_shape=[jax.ShapeDtypeStruct(shape, bf)...  84.8 us
    pallas_call x1, Pallas kernels, gather_weights(): pl.pallas_call(functools.partial(gather_kernel, count, plan), out_shape=[...  67.6 us
    reshape x5, local copies, waits for them, and re-layouts, toeplitz(): return flat.reshape(head_count, row_count, span - 1)[:, :, :key_count]  66.8 us
    another operation x10, local copies, waits for them, and re-layouts, toeplitz(): tiled = jnp.tile(reverse, (1, row_count + 1))  52.4 us
    all_gather x1, waiting for transfers between devices, body(): lax.all_gather(cross_pair[1], 'ctx', axis=1, tiled=True)  44 us
    all_gather x1, waiting for transfers between devices, body(): lax.all_gather(cross_pair[0], 'ctx', axis=1, tiled=True)  42.7 us
  transfers between devices with their start and end apart: 8, of which 6 were waited for; matrix products, arithmetic and copies ran while one was open for 18% of the time, Pallas kernels for 0%

profile of v1, /device:TPU:1, one launch (start us, length us, event | category | flops | bytes accessed | tf_op | source)
XLA Modules:
  0.0 1091.2 jit_solution(1634216389531823224)
XLA Ops:
  9.0 67.6 %gather_weights.1 = (bf16[4,2,96,768]{3,2,1,0:T(8,128)(2,1)}, bf16[4,2,96,768]{3,2,1,0:T(8,128)(2,1)}, bf16[4,2,96,768]{3,2,1,0:T(8,128)(2,1)}, bf16[4,2,96,768]...) custom-call(bf16[96,768]{1,0:T(8,128)(2,1)} %refs_0_.1, ...), custom_call_target="tpu_custom_call" | custom-call | tf_op jit(solution)/shard_map/gather_weights/pallas_call | solution.py:186
  92.9 17.8 %tile.37 = f32[12,280575]{1,0:T(8,128)} reshape(f32[12,129,2175]{2,1,0:T(8,128)} %tile.36) | data formatting | bytes 26935200 | tf_op jit(solution)/shard_map/tile | solution.py:532
  110.7 13.6 %slice.71 = f32[12,278272]{1,0:T(8,128)} slice(f32[12,280575]{1,0:T(8,128)} %tile.37), slice={[0:12], [127:278399]} | slice | bytes 26714112 | tf_op jit(solution)/shard_map/slice | solution.py:533
  124.4 37.7 %reshape.928 = f32[12,128,2174]{2,1,0:T(8,128)} reshape(f32[12,278272]{1,0:T(8,128)} %slice.71) | data formatting | bytes 26714112 | tf_op jit(solution)/shard_map/reshape | solution.py:534
  163.8 8.1 fusion.132
  181.9 8.7 fusion.133
  191.8 42.7 %all-gather.9.cloned.1.call-done = bf16[1,2048,12,64]{1,3,2,0:T(8,128)(2,1)} async-done(((bf16[1,128,12,64]{1,3,2,0:T(8,128)(2,1)}), bf16[1,2048,12,64]{1,3,2,0:T(8,128)(2,1)}) %all-gather.9.cloned.1.call-update) | async-done | bytes 3145744 | tf_op jit(solution)/shard_map/all_gather | solution.py:734
  242.9 44.0 %all-gather.11.cloned.1.call-done = bf16[1,2048,12,64]{1,3,2,0:T(8,128)(2,1)} async-done(((bf16[1,128,12,64]{1,3,2,0:T(8,128)(2,1)}), bf16[1,2048,12,64]{1,3,2,0:T(8,128)(2,1)}) %all-gather.11.cloned.1.call-update) | async-done | bytes 3145744 | tf_op jit(solution)/shard_map/all_gather | solution.py:735
  286.9 8.0 fusion.135
  310.0 48.6 %while.42 = (s32[]{:T(128)}, f32[1,128,12,64]{1,3,2,0:T(8,128)}, bf16[1,2048,12,64]{1,3,2,0:T(8,128)(2,1)}, bf16[1,2048,12,64]{1,3,2,0:T(8,128)(2,1)}, bf16[1,20...) while((s32[]{:T(128)}, f32[1,128,12,64]{1,3,2,0:T(8,128)}, ...), condition=%wide.region_10.11_spmd.clone, body=%wide.region_9.10_spmd.clone.sunk | while | flops 508231680 | bytes 52711724 | solution.py:651
  371.0 250.9 %while.43 = (s32[]{:T(128)}, f32[1,128,12,64]{1,3,2,0:T(8,128)}, bf16[1,2048,12,64]{1,3,2,0:T(8,128)(2,1)}, bf16[1,2048,12,64]{1,3,2,0:T(8,128)(2,1)}, f32[12,10...) while((s32[]{:T(128)}, f32[1,128,12,64]{1,3,2,0:T(8,128)}, ...), condition=%wide.region_15.16_spmd.clone, body=%wide.region_13.15_spmd.clone.sunk | while | flops 511062656 | bytes 128109160 | solution.py:651
  621.8 10.5 copy.118
  632.4 11.1 %reshape.974 = bf16[2048,768]{1,0:T(8,128)(2,1)} reshape(bf16[2048,1,12,64]{3,2,1,0:T(8,128)(2,1)} %bitcast.385) | data formatting | bytes 6291456
  645.4 8.7 copy.120
  654.1 11.3 %reshape.976 = bf16[2048,768]{1,0:T(8,128)(2,1)} reshape(bf16[2048,1,12,64]{3,2,1,0:T(8,128)(2,1)} %bitcast.386) | data formatting | bytes 6291456
  667.3 8.7 copy.122
  676.1 11.1 %reshape.978 = bf16[2048,768]{1,0:T(8,128)(2,1)} reshape(bf16[2048,1,12,64]{3,2,1,0:T(8,128)(2,1)} %bitcast.387) | data formatting | bytes 6291456
  689.2 8.7 copy.124
  697.9 11.2 %reshape.980 = bf16[2048,768]{1,0:T(8,128)(2,1)} reshape(bf16[2048,1,12,64]{3,2,1,0:T(8,128)(2,1)} %bitcast.388) | data formatting | bytes 6291456
  730.6 62.9 %reduce-scatter.15.cloned.1.call-done = bf16[128,768]{1,0:T(8,128)(2,1)} async-done(((bf16[2048,768]{1,0:T(8,128)(2,1)}), bf16[128,768]{1,0:T(8,128)(2,1)}) %reduce-scatter.15.cloned.1.call-update) | async-done | bytes 196624
  795.8 76.1 %reduce-scatter.17.cloned.1.call-done = bf16[128,768]{1,0:T(8,128)(2,1)} async-done(((bf16[2048,768]{1,0:T(8,128)(2,1)}), bf16[128,768]{1,0:T(8,128)(2,1)}) %reduce-scatter.17.cloned.1.call-update) | async-done | bytes 196624
  874.2 76.1 %reduce-scatter.19.cloned.1.call-done = bf16[128,768]{1,0:T(8,128)(2,1)} async-done(((bf16[2048,768]{1,0:T(8,128)(2,1)}), bf16[128,768]{1,0:T(8,128)(2,1)}) %reduce-scatter.19.cloned.1.call-update) | async-done | bytes 196624
  964.3 15.2 %outer_products.1 = bf16[2,6,4,2,2,4,16,768]{7,6,5,4,3,2,1,0:T(8,128)(2,1)} custom-call(bf16[8,128,768]{2,1,0:T(8,128)(2,1)} %get-tuple-element.893.acts, bf16[8,128,768]{2,1,0:T(8,128)(2,1)S(1)} %get-tuple-element.892.grads, bf16[128,768]{1,0:T(8,128)(2,1)S(1)} %copy-done.3, bf16[128,2048]{1,0:T(8,128)(2,1)S(1)} %copy-done.7, ...), custom_call_target="tpu_custom_call" | custom-call | tf_op jit(solution)/shard_map/outer_products/pallas_call | solution.py:471
  980.1 84.8 %reduce_weights.1 = (bf16[96,768]{1,0:T(8,128)(2,1)}, bf16[96,768]{1,0:T(8,128)(2,1)}, bf16[96,768]{1,0:T(8,128)(2,1)}, bf16[96,768]{1,0:T(8,128)(2,1)}, bf16[96...) custom-call(bf16[2,6,4,4,4,16,768]{6,5,4,3,2,1,0:T(8,128)(2,1)} %bit, ...), custom_call_target="tpu_custom_call" | custom-call | tf_op jit(solution)/shard_map/reduce_weights/pallas_call | solution.py:416
  (468 shorter events, 430.1 us)
Async XLA Ops:
  7.2 77.4 %copy-start = (f32[32,12]{0,1:T(8,128)S(1)}, f32[32,12]{0,1:T(8,128)}, u32[]{:S(2)}) copy-start(f32[32,12]{0,1:T(8,128)} %param.27) | copy-start | bytes 4612
  7.2 72.2 %copy-start.16 = (bf16[1,128,768]{2,1,0:T(8,128)(2,1)S(1)}, bf16[1,128,768]{2,1,0:T(8,128)(2,1)}, u32[]{:S(2)}) copy-start(bf16[1,128,768]{2,1,0:T(8,128)(2,1)} %param.23) | copy-start | bytes 589828
  7.2 72.2 %copy-start.65 = (f32[768]{0:T(1024)S(1)}, f32[768]{0:T(1024)}, u32[]{:S(2)}) copy-start(f32[768]{0:T(1024)} %param.28) | copy-start | bytes 9220
  7.2 156.6 %all-gather.5.cloned.1.call-start = ((), (), s32[]{:S(2)}) async-start(), calls=%async_computation.4 | async-start | bytes 3342336 | tf_op jit(solution)/shard_map/all_gather | solution.py:715
  8.9 153.4 %copy-start.73 = (f32[128]{0:T(128)}, f32[128]{0:T(128)S(1)}, u32[]{:S(2)}) copy-start(f32[128]{0:T(128)S(1)} %fusion.124) | copy-start | bytes 1540
  8.9 73.0 %copy-start.45 = (bf16[1,128,768]{2,1,0:T(8,128)(2,1)S(1)}, bf16[1,128,768]{2,1,0:T(8,128)(2,1)}, u32[]{:S(2)}) copy-start(bf16[1,128,768]{2,1,0:T(8,128)(2,1)} %param.24) | copy-start | bytes 589828
  79.3 102.6 %all-gather.7.cloned.1.call-start = ((), (), s32[]{:S(2)}) async-start(), calls=%async_computation.5 | async-start | bytes 3342336 | tf_op jit(solution)/shard_map/all_gather | solution.py:716
  81.9 152.6 %all-gather.9.cloned.1.call-start = ((), (), s32[]{:S(2)}) async-start(), calls=%async_computation.6 | async-start | bytes 3342336 | tf_op jit(solution)/shard_map/all_gather | solution.py:734
  83.2 203.7 %all-gather.11.cloned.1.call-start = ((), (), s32[]{:S(2)}) async-start(), calls=%async_computation.7 | async-start | bytes 3342336 | tf_op jit(solution)/shard_map/all_gather | solution.py:735
  84.5 643.8 %reduce-scatter.13.cloned.1.call-start = ((), (), s32[]{:S(2)}) async-start(), calls=%async_computation.8 | async-start | bytes 3342336
  124.4 38.0 %copy-start.40 = (bf16[4,2,96,768]{3,2,1,0:T(8,128)(2,1)S(1)}, bf16[4,2,96,768]{3,2,1,0:T(8,128)(2,1)}, u32[]{:S(2)}) copy-start(bf16[4,2,96,768]{3,2,1,0:T(8,128)(2,1)} %get-tuple-element.631) | copy-start | bytes 3538948
  191.1 47.2 %copy-start.81 = (f32[128]{0:T(128)}, f32[128]{0:T(128)S(1)}, u32[]{:S(2)}) copy-start(f32[128]{0:T(128)S(1)} %get-tuple-element.881) | copy-start | bytes 1540
  191.1 103.9 %copy-start.18 = (f32[1,128,768]{2,1,0:T(8,128)}, f32[1,128,768]{2,1,0:T(8,128)S(1)}, u32[]{:S(2)}) copy-start(f32[1,128,768]{2,1,0:T(8,128)S(1)} %get-tuple-element.882) | copy-start | bytes 1179652
  191.1 47.2 %copy-start.77 = (f32[128]{0:T(128)}, f32[128]{0:T(128)S(1)}, u32[]{:S(2)}) copy-start(f32[128]{0:T(128)S(1)} %fusion.125) | copy-start | bytes 1540
  242.9 52.0 %copy-start.43 = (bf16[4,2,96,768]{3,2,1,0:T(8,128)(2,1)S(1)}, bf16[4,2,96,768]{3,2,1,0:T(8,128)(2,1)}, u32[]{:S(2)}) copy-start(bf16[4,2,96,768]{3,2,1,0:T(8,128)(2,1)} %get-tuple-element.638) | copy-start | bytes 3538948
  242.9 52.5 %copy-start.72 = (f32[768]{0:T(1024)S(1)}, f32[768]{0:T(1024)}, u32[]{:S(2)}) copy-start(f32[768]{0:T(1024)} %param.30) | copy-start | bytes 9220
  643.5 150.0 %reduce-scatter.15.cloned.1.call-start = ((), (), s32[]{:S(2)}) async-start(), calls=%async_computation.9 | async-start | bytes 3342336
  665.5 206.5 %reduce-scatter.17.cloned.1.call-start = ((), (), s32[]{:S(2)}) async-start(), calls=%async_computation.10 | async-start | bytes 3342336
  687.2 263.1 %reduce-scatter.19.cloned.1.call-start = ((), (), s32[]{:S(2)}) async-start(), calls=%async_computation.11 | async-start | bytes 3342336
  729.6 224.6 %copy-start.33 = (f32[1,128,768]{2,1,0:T(8,128)S(1)}, f32[1,128,768]{2,1,0:T(8,128)}, u32[]{:S(2)}) copy-start(f32[1,128,768]{2,1,0:T(8,128)} %copy-done.32) | copy-start | bytes 1179652
  964.3 15.2 %copy-start.75 = (f32[768]{0:T(1024)S(1)}, f32[768]{0:T(1024)}, u32[]{:S(2)}) copy-start(f32[768]{0:T(1024)} %get-tuple-element.817) | copy-start | bytes 9220
  980.1 87.0 %copy-start.80 = (f32[128]{0:T(128)S(1)}, f32[128]{0:T(128)}, u32[]{:S(2)}) copy-start(f32[128]{0:T(128)} %copy-done.79) | copy-start | bytes 1540
  980.1 87.0 %copy-start.39 = (bf16[4,2,96,768]{3,2,1,0:T(8,128)(2,1)S(1)}, bf16[4,2,96,768]{3,2,1,0:T(8,128)(2,1)}, u32[]{:S(2)}) copy-start(bf16[4,2,96,768]{3,2,1,0:T(8,128)(2,1)} %get-tuple-element.636) | copy-start | bytes 3538948
  980.1 87.0 %copy-start.52 = (bf16[1,128,12,64]{1,3,2,0:T(8,128)(2,1)S(1)}, bf16[1,128,12,64]{1,3,2,0:T(8,128)(2,1)}, u32[]{:S(2)}) copy-start(bf16[1,128,12,64]{1,3,2,0:T(8,128)(2,1)} %copy.123) | copy-start | bytes 589828
  (90 other events, 474.9 us)
Sparse Core Ops, SparseCore 0:
  79.5 49.8 all-gather.4
  132.2 49.6 all-gather.6
  184.8 49.6 all-gather.8
  237.2 49.6 all-gather.10
  643.7 71.5 reduce-scatter.12
  719.2 74.2 reduce-scatter.14
  797.6 74.3 reduce-scatter.16
  876.0 74.3 reduce-scatter.18

commit v2 on v1

--- a/solution.py
+++ b/solution.py
@@ -489,8 +489,483 @@
         name="outer_products",
     )(acts, grads, third, gate, up, mixed_cut, cot)
     return out.reshape(2, 6, 4, 4, 4, 16, 768)
+
+NEGATIVE = -1e30
+TILES = 23
+USED = 16
+
+
+class Share(Place):
+    def __init__(self):
+        super().__init__()
+        self.dev["zab"] = (self.x_hi * 8 + self.z_ab * 2 + self.core, self.d)
+        self.mine = self.x_hi * 2 + self.core
+        self.slot = self.c // 4
+        rest = self.c % 4
+        self.owner = rest + (self.slot % 2) * (3 - 2 * rest)
+        self.at_home = self.owner == self.mine
+
+    def block(self, slot):
+        return 4 * slot + (self.mine if slot % 2 == 0 else 3 - self.mine)
+
+    def worker(self, group):
+        return (self.owner // 2) * 8 + group * 2 + self.owner % 2
+
+    def greet_all(self):
+        barrier = pltpu.get_barrier_semaphore()
+        for step in range(1, 16):
+            pl.semaphore_signal(
+                barrier, inc=1, device_id=((self.c + step) % 16, self.d), device_id_type=MESH
+            )
+        pl.semaphore_wait(barrier, 15)
+
+    def copy_to(self, ctx, src, dst, send_sem, recv_sem):
+        return pltpu.make_async_remote_copy(
+            src_ref=src,
+            dst_ref=dst,
+            send_sem=send_sem,
+            recv_sem=recv_sem,
+            device_id=(ctx, self.d),
+            device_id_type=MESH,
+        )
+
+
+def spread_kernel(q_count, kv_count, *refs):
+    n = q_count + kv_count
+    ins, outs = refs[:n], refs[n : 2 * n]
+    q_send, q_recv, kv_send, kv_recv = refs[2 * n :]
+    me = Share()
+    me.greet_all()
+    groups = (me.z_a, me.z_b, me.z_ab)
+    done = []
+
+    def go(name, src, dst, index, slot):
+        copy = me.send(name, src, dst, kv_send.at[index, slot], kv_recv.at[index, slot])
+        done.append(copy)
+        return copy
+
+    first = []
+    for index in range(kv_count):
+        src, out = ins[q_count + index], outs[q_count + index]
+        out[me.c] = src[me.z]
+        across = [
+            go(name, src.at[group], out.at[me.c], index, slot)
+            for slot, (name, group) in enumerate(zip(("za", "zb", "zab"), groups))
+        ]
+        first.append(across)
+    for index in range(q_count):
+        src, out = ins[index], outs[index]
+        for group in range(4):
+            away = jnp.logical_not(jnp.logical_and(me.at_home, me.z == group))
+
+            @pl.when(away)
+            def _():
+                me.copy_to(
+                    me.worker(group), src.at[group], out.at[me.slot],
+                    q_send.at[index, group], q_recv.at[index, me.slot],
+                ).start()
+
+        @pl.when(me.at_home)
+        def _():
+            out[me.slot] = src[me.z]
+
+    second = []
+    for index in range(kv_count):
+        out = outs[q_count + index]
+        pairs = []
+        for step, group in enumerate((me.z,) + groups):
+            if step:
+                first[index][step - 1].wait_recv()
+            block = me.x_hi * 8 + group * 2 + me.core
+            pairs.append(go("xab", out.at[block], out.at[block], index, 3 + step))
+            pairs.append(go("core", out.at[block], out.at[block], index, 7 + step))
+        second.append(pairs)
+    third = []
+    for index in range(kv_count):
+        out = outs[q_count + index]
+        for step, group in enumerate((me.z,) + groups):
+            second[index][2 * step].wait_recv()
+            block = (1 - me.x_hi) * 8 + group * 2 + me.core
+            third.append(go("core", out.at[block], out.at[block], index, 11 + step))
+    for pairs in second:
+        for copy in pairs[1::2]:
+            copy.wait_recv()
+    for copy in third:
+        copy.wait_recv()
+    for index in range(q_count):
+        src, out = ins[index], outs[index]
+        for group in range(4):
+            away = jnp.logical_not(jnp.logical_and(me.at_home, me.z == group))
+
+            @pl.when(away)
+            def _():
+                me.copy_to(
+                    me.worker(group), src.at[group], out.at[me.slot],
+                    q_send.at[index, group], q_recv.at[index, me.slot],
+                ).wait_send()
+
+        for slot in range(4):
+            @pl.when(me.block(slot) != me.c)
+            def _():
+                me.copy_to(
+                    me.block(slot), src.at[0], out.at[slot],
+                    q_send.at[index, 0], q_recv.at[index, slot],
+                ).wait_recv()
+
+    for copy in done:
+        copy.wait_send()
+
+
+def spread(q_list, kv_list, collective_id):
+    nq, nkv = len(q_list), len(kv_list)
+    return pl.pallas_call(
+        functools.partial(spread_kernel, nq, nkv),
+        out_shape=[jax.ShapeDtypeStruct((4, 128, 256), jnp.bfloat16)] * nq
+        + [jax.ShapeDtypeStruct((16, 128, 384), jnp.bfloat16)] * nkv,
+        in_specs=[VMEM] * (nq + nkv),
+        out_specs=[VMEM] * (nq + nkv),
+        scratch_shapes=[
+            pltpu.SemaphoreType.DMA((max(nq, 1), 4)),
+            pltpu.SemaphoreType.DMA((max(nq, 1), 4)),
+            pltpu.SemaphoreType.DMA((max(nkv, 1), 15)),
+            pltpu.SemaphoreType.DMA((max(nkv, 1), 15)),
+        ],
+        compiler_params=pltpu.CompilerParams(
+            collective_id=collective_id, has_side_effects=True, vmem_limit_bytes=32 * 2**20
+        ),
+        name="spread_%d_%d" % (nq, nkv),
+    )(*q_list, *kv_list)
+
+
+def collect_kernel(with_kv, *refs):
+    if with_kv:
+        (o_in, kv_in, o_out, kv_out, o_send, o_recv, kv_send, kv_recv,
+         got_core, part, got_x, total) = refs
+    else:
+        o_in, o_out, o_send, o_recv = refs
+    me = Share()
+    me.greet_all()
+    done = []
+    if with_kv:
+        def go(name, src, dst, slot):
+            copy = me.send(name, src, dst, kv_send.at[slot], kv_recv.at[slot])
+            done.append(copy)
+            return copy
+
+        near, far = me.x_hi * 4, (1 - me.x_hi) * 4
+        to_core = [
+            go("core", kv_in.at[pl.ds(begin, 4), 1 - me.core], got_core.at[pl.ds(begin, 4)], slot)
+            for slot, begin in enumerate((far, near))
+        ]
+    for slot in range(4):
+        @pl.when(me.block(slot) != me.c)
+        def _():
+            me.copy_to(
+                me.block(slot), o_in.at[slot], o_out.at[me.z], o_send.at[slot], o_recv.at[me.z]
+            ).start()
+
+    @pl.when(me.at_home)
+    def _():
+        o_out[me.z] = o_in[me.slot]
+
+    if with_kv:
+        to_core[0].wait_recv()
+        part[pl.ds(far, 4)] = kv_in[pl.ds(far, 4), me.core] + got_core[pl.ds(far, 4)]
+        over_x = go("xab", part.at[pl.ds(far, 4)], got_x, 2)
+        to_core[1].wait_recv()
+        part[pl.ds(near, 4)] = kv_in[pl.ds(near, 4), me.core] + got_core[pl.ds(near, 4)]
+        over_x.wait_recv()
+        total[...] = part[pl.ds(near, 4)] + got_x[...]
+        across = [
+            go(name, total.at[group], kv_out.at[me.z], 3 + step)
+            for step, (name, group) in enumerate(
+                zip(("za", "zb", "zab"), (me.z_a, me.z_b, me.z_ab))
+            )
+        ]
+        kv_out[me.z] = total[me.z]
+        for copy in across:
+            copy.wait_recv()
+    for slot in range(4):
+        @pl.when(me.block(slot) != me.c)
+        def _():
+            me.copy_to(
+                me.block(slot), o_in.at[slot], o_out.at[me.z], o_send.at[slot], o_recv.at[me.z]
+            ).wait_send()
+
+    for group in range(4):
+        away = jnp.logical_not(jnp.logical_and(me.at_home, me.z == group))
+
+        @pl.when(away)
+        def _():
+            me.copy_to(
+                me.worker(group), o_in.at[0], o_out.at[group], o_send.at[0], o_recv.at[group]
+            ).wait_recv()
+
+    for copy in done:
+        copy.wait_send()
+
+
+def collect(rows, pairs, collective_id):
+    bf = jnp.bfloat16
+    with_kv = pairs is not None
+    shapes = [jax.ShapeDtypeStruct((4, 128, 256), bf)]
+    scratch = [pltpu.SemaphoreType.DMA((4,)), pltpu.SemaphoreType.DMA((4,))]
+    args = [rows]
+    if with_kv:
+        shapes.append(jax.ShapeDtypeStruct((4, 128, 384), bf))
+        args.append(pairs.reshape(8, 2, 128, 384))
+        scratch += [
+            pltpu.SemaphoreType.DMA((6,)),
+            pltpu.SemaphoreType.DMA((6,)),
+            pltpu.VMEM((8, 128, 384), bf),
+            pltpu.VMEM((8, 128, 384), bf),
+            pltpu.VMEM((4, 128, 384), bf),
+            pltpu.VMEM((4, 128, 384), bf),
+        ]
+    return pl.pallas_call(
+        functools.partial(collect_kernel, with_kv),
+        out_shape=shapes,
+        in_specs=[VMEM] * len(args),
+        out_specs=[VMEM] * len(shapes),
+        scratch_shapes=scratch,
+        compiler_params=pltpu.CompilerParams(
+            collective_id=collective_id, has_side_effects=True, vmem_limit_bytes=32 * 2**20
+        ),
+        name="collect_kv" if with_kv else "collect",
+    )(*args)
+
+
+def dot_nn(left, right):
+    return jnp.dot(left, right, preferred_element_type=jnp.float32)
+
+
+def dot_nt(left, right):
+    return lax.dot_general(
+        left, right, (((1,), (1,)), ((), ())), preferred_element_type=jnp.float32
+    )
+
+
+def head_lanes(value, head):
+    lane = lax.broadcasted_iota(jnp.int32, value.shape, 1)
+    return jnp.where(lane // 64 == head, value, jnp.zeros_like(value))
+
+
+def head_rows(value, head):
+    row = lax.broadcasted_iota(jnp.int32, value.shape, 0)
+    return jnp.where(row // 64 == head, value, jnp.zeros_like(value))
+
+
+def bias_offset(pair, side, chunk):
+    c = lax.axis_index("ctx")
+    mine = (c // 8) * 2 + c % 2
+    block = 8 * pair + (mine if side == 0 else 7 - mine)
+    return pl.multiple_of((15 - block) * 128 + chunk * 256, 128)
+
+
+def bias_at(wide, head, pair, chunk):
+    return jnp.concatenate(
+        [wide[head, pl.ds(bias_offset(pair, side, chunk), 256), :] for side in range(2)], axis=1
+    )
+
+
+def forward_kernel(causal, *refs):
+    if causal:
+        q, kv, waves, o_low, o_full, lse, wide, values_t, score, total = refs
+        def build(head, carry):
+            for tile in range(USED):
+                row = jnp.broadcast_to(waves[head, tile : tile + 1, :], (128, 256))
+                turned = pltpu.roll(row, 129, 1, stride=1, stride_axis=0)
+                wide[head, tile * 128 : tile * 128 + 128, :] = turned[:, :128]
+            wide[head, USED * 128 :, :] = jnp.full(
+                ((TILES - USED) * 128, 128), NEGATIVE, jnp.float32
+            )
+            return carry
+
+        lax.fori_loop(0, 3, build, 0)
+    else:
+        q, kv, o_low, o_full, lse, values_t, score, total = refs
+
+    for chunk in range(8):
+        values_t[chunk] = kv[2 * chunk : 2 * chunk + 2, :, 128:384].reshape(256, 256).T
+    for pair in range(2):
+        chunks = 4 if causal and pair == 0 else 8
+        rows = q[2 * pair : 2 * pair + 2].reshape(256, 256)
+        total[...] = jnp.zeros_like(total)
+
+        def one_head(head, carry):
+            masked = head_lanes(rows, head)
+
+            top = jnp.full((8, 256), NEGATIVE, jnp.float32)
+            for chunk in range(chunks):
+                keys = kv[2 * chunk : 2 * chunk + 2, :, 0:256].reshape(256, 256)
+                block = dot_nt(keys, masked)
+                if causal:
+                    block = block + bias_at(wide, head, pair, chunk)
+                score[chunk] = block
+                top = jnp.maximum(top, jnp.max(block.reshape(32, 8, 256), axis=0))
+            top = jnp.max(top, axis=0, keepdims=True)
+            summed = jnp.zeros((8, 256), jnp.float32)
+            held = jnp.zeros((256, 256), jnp.float32)
+            for chunk in range(chunks):
+                expo = jnp.exp(score[chunk] - top)
+                summed = summed + jnp.sum(expo.reshape(32, 8, 256), axis=0)
+                held = held + dot_nn(values_t[chunk], expo.astype(jnp.bfloat16))
+            summed = jnp.sum(summed, axis=0, keepdims=True)
+            total[...] += head_rows(held * (1.0 / summed), head + 1)
+            lse[head, pair] = top + jnp.log(summed)
+            return carry
+
+        lax.fori_loop(0, 3, one_head, 0)
+        final = total[...].T.reshape(2, 128, 256)
+        o_full[2 * pair : 2 * pair + 2] = final
+        o_low[2 * pair : 2 * pair + 2] = final.astype(jnp.bfloat16)
+
+
+def attend(q, kv, waves):
+    causal = waves is not None
+    shapes = [
+        jax.ShapeDtypeStruct((4, 128, 256), jnp.bfloat16),
+        jax.ShapeDtypeStruct((4, 128, 256), jnp.float32),
+        jax.ShapeDtypeStruct((3, 2, 1, 256), jnp.float32),
+    ]
+    args = [q, kv]
+    if causal:
+        shapes.append(jax.ShapeDtypeStruct((3, TILES * 128, 128), jnp.float32))
+        args.append(waves)
+    return pl.pallas_call(
+        functools.partial(forward_kernel, causal),
+        out_shape=shapes,
+        in_specs=[VMEM] * len(args),
+        out_specs=[VMEM] * len(shapes),
+        scratch_shapes=[
+            pltpu.VMEM((8, 256, 256), jnp.bfloat16),
+            pltpu.VMEM((8, 256, 256), jnp.float32),
+            pltpu.VMEM((256, 256), jnp.float32),
+        ],
+        compiler_params=pltpu.CompilerParams(vmem_limit_bytes=40 * 2**20),
+        name="attend_self" if causal else "attend_cross",
+    )(*args)
+
+
+def backward_kernel(causal, *refs):
+    if causal:
+        (q, kv, grad, o_full, lse, wide, dq, dkv, waves,
+         keys_t, dk, dv, dq_t, turned, along) = refs
+        along[...] = jnp.zeros_like(along)
+    else:
+        q, kv, grad, o_full, lse, dq, dkv, keys_t, dk, dv, dq_t, turned = refs
+    dk[...] = jnp.zeros_like(dk)
+    dv[...] = jnp.zeros_like(dv)
+
+    for chunk in range(8):
+        keys_t[chunk] = kv[2 * chunk : 2 * chunk + 2, :, 0:256].reshape(256, 256).T
+    for pair in range(2):
+        chunks = 4 if causal and pair == 0 else 8
+        both = slice(2 * pair, 2 * pair + 2)
+        rows = q[both].reshape(256, 256)
+        grads = grad[both].reshape(256, 256)
+        turned[...] = (grads.astype(jnp.float32) * o_full[both].reshape(256, 256)).T
+        dq_t[...] = jnp.zeros_like(dq_t)
+
+        def one_head(head, carry):
+            masked = head_lanes(rows, head)
+            masked_grads = head_lanes(grads, head + 1)
+            delta = jnp.sum(head_rows(turned[...], head + 1), axis=0, keepdims=True)
+            row_lse = lse[head, pair]
+
+            held = jnp.zeros((256, 256), jnp.float32)
+            for chunk in range(chunks):
+                block = kv[2 * chunk : 2 * chunk + 2].reshape(256, 384)
+                scores = dot_nt(block[:, 0:256], masked)
+                if causal:
+                    scores = scores + bias_at(wide, head, pair, chunk)
+                probs = jnp.exp(scores - row_lse)
+                grad_probs = dot_nt(block[:, 128:384], masked_grads)
+                grad_scores = probs * (grad_probs - delta)
+                low = grad_scores.astype(jnp.bfloat16)
+                spot = slice(chunk * 256, chunk * 256 + 256)
+                dk[spot] += dot_nn(low, masked)
+                dv[spot] += dot_nn(probs.astype(jnp.bfloat16), masked_grads)
+                if causal:
+                    for side in range(2):
+                        where = pl.ds(bias_offset(pair, side, chunk), 256)
+                        along[head, where, :] += grad_scores[:, 128 * side : 128 * side + 128]
+                held = held + dot_nn(keys_t[chunk], low)
+            dq_t[...] += head_rows(held, head)
+            return carry
+
+        lax.fori_loop(0, 3, one_head, 0)
+        dq[both] = dq_t[...].T.reshape(2, 128, 256).astype(jnp.bfloat16)
+
+    def pack(block, carry):
+        spot = pl.ds(pl.multiple_of(block * 128, 128), 128)
+        key_part, value_part = dk[spot], dv[spot]
+        dkv[block, :, 0:128] = key_part[:, 0:128].astype(jnp.bfloat16)
+        dkv[block, :, 128:256] = (key_part[:, 128:256] + value_part[:, 0:128]).astype(jnp.bfloat16)
+        dkv[block, :, 256:384] = value_part[:, 128:256].astype(jnp.bfloat16)
+        return carry
+
+    lax.fori_loop(0, 16, pack, 0)
+    if causal:
+        waves[...] = jnp.zeros_like(waves)
+
+        def fold(head, carry):
+            for tile in range(USED):
+                value = along[head, tile * 128 : tile * 128 + 128, :]
+                value = jnp.concatenate([value, jnp.zeros_like(value)], axis=1)
+                count = 64
+                while count >= 1:
+                    value = pltpu.roll(value[:count], count, 1) + value[count:]
+                    count //= 2
+                waves[head, tile : tile + 1, :] = value
+            return carry
+
+        lax.fori_loop(0, 3, fold, 0)
+
+
+def attend_back(q, kv, grad, o_full, lse, wide):
+    causal = wide is not None
+    shapes = [
+        jax.ShapeDtypeStruct((4, 128, 256), jnp.bfloat16),
+        jax.ShapeDtypeStruct((16, 128, 384), jnp.bfloat16),
+    ]
+    args = [q, kv, grad, o_full, lse]
+    scratch = [
+        pltpu.VMEM((8, 256, 256), jnp.bfloat16),
+        pltpu.VMEM((2048, 256), jnp.float32),
+        pltpu.VMEM((2048, 256), jnp.float32),
+        pltpu.VMEM((256, 256), jnp.float32),
+        pltpu.VMEM((256, 256), jnp.float32),
+    ]
+    if causal:
+        shapes.append(jax.ShapeDtypeStruct((3, TILES, 256), jnp.float32))
+        args.append(wide)
+        scratch.append(pltpu.VMEM((3, TILES * 128, 128), jnp.float32))
+    return pl.pallas_call(
+        functools.partial(backward_kernel, causal),
+        out_shape=shapes,
+        in_specs=[VMEM] * len(args),
+        out_specs=[VMEM] * len(shapes),
+        scratch_shapes=scratch,
+        compiler_params=pltpu.CompilerParams(vmem_limit_bytes=48 * 2**20),
+        name="attend_back_self" if causal else "attend_back_cross",
+    )(*args)
+
+
+def to_groups(activity, before):
+    cut = activity.reshape(activity.shape[0], 4, 192).transpose(1, 0, 2)
+    return jnp.pad(cut, ((0, 0), (0, 0), (64, 0) if before else (0, 64)))
+
+
+def from_groups(grouped, begin):
+    cut = grouped[:, :, begin : begin + 192].transpose(1, 0, 2)
+    return cut.reshape(cut.shape[0], 768)
+
+
+def pair_groups(keys, values):
+    cut = lambda activity: activity.reshape(activity.shape[0], 4, 192).transpose(1, 0, 2)
+    return jnp.concatenate([cut(keys), cut(values)], axis=2)
 EPSILON = 1e-06
-NEGATIVE = -1e30
 PRECISE = lax.Precision.HIGHEST
 
 
@@ -503,152 +978,11 @@
 
 
 def project(activity, weight):
-    return jnp.einsum("scd,df->scf", activity, weight, preferred_element_type=jnp.float32)
+    return jnp.einsum("td,df->tf", activity, weight, preferred_element_type=jnp.float32)
 
 
 def project_back(gradient, weight):
-    return jnp.einsum("scf,df->scd", gradient, weight, preferred_element_type=jnp.float32)
-
-
-def outer_sum(activity, gradient):
-    return jnp.einsum("scd,scf->df", activity, gradient, preferred_element_type=jnp.float32)
-
-
-def split_heads(activity, head_count):
-    return activity.reshape(
-        activity.shape[0], activity.shape[1], head_count, activity.shape[2] // head_count
-    )
-
-
-def join_heads(activity):
-    return activity.reshape(
-        activity.shape[0], activity.shape[1], activity.shape[2] * activity.shape[3]
-    )
-
-
-def toeplitz(vector, row_count, key_count):
-    head_count, span = vector.shape
-    reverse = vector[:, ::-1]
-    tiled = jnp.tile(reverse, (1, row_count + 1))
-    flat = tiled[:, row_count - 1 : row_count - 1 + row_count * (span - 1)]
-    return flat.reshape(head_count, row_count, span - 1)[:, :, :key_count]
-
-
-def diagonal_sums(block, span):
-    head_count, row_count, key_count = block.shape
-    widened = jnp.pad(block, ((0, 0), (0, 0), (0, span - 1 - key_count)))
-    widened = widened.reshape(head_count, row_count * (span - 1))
-    placed = jnp.pad(widened, ((0, 0), (row_count - 1, span + 1))).reshape(
-        head_count, row_count + 1, span
-    )
-    return jnp.sum(placed, axis=1)[:, ::-1]
-
-
-def causal_bias(bias_info, query_begin, row_count, key_begin, key_count):
-    bias_pad, margin = bias_info
-    span = row_count + key_count - 1
-    slice_start = margin + query_begin - key_begin - (key_count - 1)
-    vector = lax.dynamic_slice_in_dim(bias_pad, slice_start, span, 1)
-    bias_block = toeplitz(vector, row_count, key_count)[None]
-    query_pos = query_begin + jnp.arange(row_count, dtype=jnp.int32)
-    key_pos = key_begin + jnp.arange(key_count, dtype=jnp.int32)
-    allowed = (query_pos[:, None] >= key_pos[None, :])[None, None]
-    return (bias_block, allowed, slice_start)
-
-
-def make_fold(queries, query_begin, bias_info):
-
-    def fold_step(running, pieces, begin_row):
-        key_block, value_block = pieces
-        row_max, row_sum, weighted = running
-        scores = jnp.einsum(
-            "sqhe,skhe->shqk", queries, key_block, preferred_element_type=jnp.float32
-        )
-        if bias_info is not None:
-            bias_block, allowed, unused = causal_bias(
-                bias_info, query_begin, queries.shape[1], begin_row, key_block.shape[1]
-            )
-            scores = jnp.where(allowed, scores + bias_block, NEGATIVE)
-        new_max = jnp.maximum(row_max, jnp.max(scores, axis=-1))
-        unscaled = jnp.exp(scores - new_max[..., None])
-        if bias_info is not None:
-            unscaled = jnp.where(allowed, unscaled, 0.0)
-        row_sum = jnp.sum(unscaled, axis=-1)
-        weighted = jnp.einsum(
-            "shqk,skhe->shqe",
-            unscaled.astype(jnp.bfloat16),
-            value_block,
-            preferred_element_type=jnp.float32,
-        )
-        return (new_max, row_sum, weighted)
-
-    return fold_step
-
-
-def finish_rows(running):
-    row_max, row_sum, weighted = running
-    out_heads = jnp.transpose(weighted / row_sum[..., None], (0, 2, 1, 3))
-    return (out_heads, row_max + jnp.log(row_sum))
-
-
-def attend_back(queries, out_heads, grad_heads, row_lse, pair, bias_info, query_begin):
-    key_all, value_all = pair
-    seq_count, row_count, head_count, head_size = queries.shape
-    key_total = key_all.shape[1]
-    block_len = math.gcd(512, key_total)
-    span = row_count + block_len - 1
-    delta = jnp.transpose(jnp.sum(grad_heads.astype(jnp.float32) * out_heads, axis=-1), (0, 2, 1))
-
-    def back_step(block_index, running):
-        grad_query, grad_keys, grad_values, grad_offsets = running
-        begin_row = block_index * block_len
-        key_block = lax.dynamic_slice_in_dim(key_all, begin_row, block_len, 1)
-        value_block = lax.dynamic_slice_in_dim(value_all, begin_row, block_len, 1)
-        scores = jnp.einsum(
-            "sqhe,skhe->shqk", queries, key_block, preferred_element_type=jnp.float32
-        )
-        if bias_info is not None:
-            bias_block, allowed, slice_start = causal_bias(
-                bias_info, query_begin, row_count, begin_row, block_len
-            )
-            scores = jnp.where(allowed, scores + bias_block, NEGATIVE)
-        probs = jnp.exp(scores - row_lse[..., None])
-        grad_probs = jnp.einsum(
-            "sqhe,skhe->shqk", grad_heads, value_block, preferred_element_type=jnp.float32
-        )
-        grad_scores = (probs * (grad_probs - delta[..., None])).astype(jnp.bfloat16)
-        grad_query = grad_query + jnp.einsum(
-            "shqk,skhe->sqhe", grad_scores, key_block, preferred_element_type=jnp.float32
-        )
-        key_part = jnp.einsum(
-            "shqk,sqhe->skhe", grad_scores, queries, preferred_element_type=jnp.float32
-        )
-        value_part = jnp.einsum(
-            "shqk,sqhe->skhe",
-            probs.astype(jnp.bfloat16),
-            grad_heads,
-            preferred_element_type=jnp.float32,
-        )
-        grad_keys = lax.dynamic_update_slice_in_dim(grad_keys, key_part, begin_row, 1)
-        grad_values = lax.dynamic_update_slice_in_dim(grad_values, value_part, begin_row, 1)
-        if bias_info is not None:
-            summed = jnp.sum(grad_scores.astype(jnp.float32), axis=0)
-            along = diagonal_sums(summed, span)
-            current = lax.dynamic_slice_in_dim(grad_offsets, slice_start, span, 1)
-            grad_offsets = lax.dynamic_update_slice_in_dim(
-                grad_offsets, current + along, slice_start, 1
-            )
-        return (grad_query, grad_keys, grad_values, grad_offsets)
-
-    key_shape = key_all.shape
-    offset_shape = bias_info[0].shape if bias_info is not None else (1,)
-    initial = (
-        jnp.zeros(queries.shape, jnp.float32),
-        jnp.zeros(key_shape, jnp.float32),
-        jnp.zeros(key_shape, jnp.float32),
-        jnp.zeros(offset_shape, jnp.float32),
-    )
-    return lax.fori_loop(0, key_total // block_len, back_step, initial)
+    return jnp.einsum("tf,df->td", gradient, weight, preferred_element_type=jnp.float32)
 
 
 def body(
@@ -672,10 +1006,9 @@
     up_weight,
     down_weight,
 ):
-    head_count = bias_table.shape[1]
-    bucket_count = bias_table.shape[0]
-    seq_count, row_count, model_width = layer_input.shape
-    head_size = model_width // head_count
+    bucket_count, head_count = bias_table.shape
+    width = layer_input.shape[-1]
+    layer_input, encoder_states, cotangent = layer_input[0], encoder_states[0], cotangent[0]
     weights = gather_weights(
         (
             self_query, self_key, self_value, self_output,
@@ -685,119 +1018,75 @@
         GATHER_PLAN,
         0,
     )
-    position = lax.axis_index("ctx")
-    query_begin = position * row_count
-    distance_count = bucket_ids.shape[0]
-    margin = 2 * distance_count
-    table_hot = (bucket_ids[:, None] == jnp.arange(bucket_count, dtype=jnp.int32)[None, :]).astype(
-        jnp.float32
-    )
-    bias_rows = jnp.dot(table_hot, bias_table, precision=PRECISE)
-    bias_pad = jnp.pad(jnp.transpose(bias_rows), ((0, 0), (margin, margin)))
-    bias_info = (bias_pad, margin)
-    initial = (
-        jnp.full((seq_count, head_count, row_count), NEGATIVE, jnp.float32),
-        jnp.zeros((seq_count, head_count, row_count), jnp.float32),
-        jnp.zeros((seq_count, head_count, row_count, head_size), jnp.float32),
-    )
+    low = jnp.bfloat16
+    first_head = 3 * ((lax.axis_index("ctx") // 2) % 4)
+    padded = jnp.pad(bucket_ids, (TILES * 128 - bucket_ids.shape[0] + 128, 0), constant_values=-1)
+    last = padded.shape[0]
+    ids = jnp.stack([padded[last - 255 - 128 * k - 0 : last - 128 * k] for k in range(TILES)])
+    ids = jnp.pad(ids, ((0, 0), (0, 1)), constant_values=-1)
+    hot = (ids[:, :, None] == jnp.arange(bucket_count, dtype=jnp.int32)).astype(jnp.float32)
+    own_table = lax.dynamic_slice_in_dim(bias_table, first_head, 3, 1)
+    waves = jnp.einsum("kxb,bh->hkx", hot, own_table, precision=PRECISE)
+    waves = jnp.where((ids >= 0)[None], waves, NEGATIVE)
+
     residual = layer_input.astype(jnp.float32)
     normed, back_first = jax.vjp(rms_norm, residual, gain_first)
-    normed_one = normed.astype(jnp.bfloat16)
-    queries = split_heads(project(normed_one, weights[0]).astype(jnp.bfloat16), head_count)
-    self_pair = (
-        split_heads(project(normed_one, weights[1]).astype(jnp.bfloat16), head_count),
-        split_heads(project(normed_one, weights[2]).astype(jnp.bfloat16), head_count),
+    normed_one = normed.astype(low)
+    queries = project(normed_one, weights[0]).astype(low)
+    keys = project(normed_one, weights[1]).astype(low)
+    values = project(normed_one, weights[2]).astype(low)
+    cross_keys = project(encoder_states, weights[5]).astype(low)
+    cross_values = project(encoder_states, weights[6]).astype(low)
+    self_q, self_kv, cross_kv = spread(
+        [to_groups(queries, False)],
+        [pair_groups(keys, values), pair_groups(cross_keys, cross_values)],
+        2,
     )
-    self_fold = make_fold(queries, query_begin, bias_info)
-    self_state = self_fold(
-        initial,
-        (
-            lax.all_gather(self_pair[0], "ctx", axis=1, tiled=True),
-            lax.all_gather(self_pair[1], "ctx", axis=1, tiled=True),
-        ),
-        jnp.int32(0),
-    )
-    self_heads, self_lse = finish_rows(self_state)
-    attended = join_heads(self_heads).astype(jnp.bfloat16)
+    self_low, self_full, self_lse, wide = attend(self_q, self_kv, waves)
+    attended = from_groups(collect(self_low, None, 3)[0], 64)
     middle = residual + project(attended, weights[3])
     normed, back_second = jax.vjp(rms_norm, middle, gain_second)
-    normed_two = normed.astype(jnp.bfloat16)
-    cross_queries = split_heads(project(normed_two, weights[4]).astype(jnp.bfloat16), head_count)
-    cross_pair = (
-        split_heads(project(encoder_states, weights[5]).astype(jnp.bfloat16), head_count),
-        split_heads(project(encoder_states, weights[6]).astype(jnp.bfloat16), head_count),
-    )
-    cross_fold = make_fold(cross_queries, query_begin, None)
-    cross_state = cross_fold(
-        initial,
-        (
-            lax.all_gather(cross_pair[0], "ctx", axis=1, tiled=True),
-            lax.all_gather(cross_pair[1], "ctx", axis=1, tiled=True),
-        ),
-        jnp.int32(0),
-    )
-    cross_heads, cross_lse = finish_rows(cross_state)
-    crossed = join_heads(cross_heads).astype(jnp.bfloat16)
+    normed_two = normed.astype(low)
+    cross_queries = project(normed_two, weights[4]).astype(low)
+    (cross_q,) = spread([to_groups(cross_queries, False)], [], 4)
+    cross_low, cross_full, cross_lse = attend(cross_q, cross_kv, None)
+    crossed = from_groups(collect(cross_low, None, 5)[0], 64)
     after_cross = middle + project(crossed, weights[7])
     normed, back_third = jax.vjp(rms_norm, after_cross, gain_third)
-    normed_three = normed.astype(jnp.bfloat16)
+    normed_three = normed.astype(low)
     gate_act = project(normed_three, weights[8])
     up_act = project(normed_three, weights[9])
     mixed_act, back_mix = jax.vjp(gated_gelu, gate_act, up_act)
-    mixed_low = mixed_act.astype(jnp.bfloat16)
-    final = after_cross + project(mixed_low, weights[10])
-    layer_output = final.astype(jnp.bfloat16)
+    mixed_low = mixed_act.astype(low)
+    layer_output = (after_cross + project(mixed_low, weights[10])).astype(low)
+
     grad_gate, grad_up = back_mix(project_back(cotangent, weights[10]))
-    grad_gate = grad_gate.astype(jnp.bfloat16)
-    grad_up = grad_up.astype(jnp.bfloat16)
+    grad_gate = grad_gate.astype(low)
+    grad_up = grad_up.astype(low)
     grad_normed = project_back(grad_gate, weights[8]) + project_back(grad_up, weights[9])
     grad_back, grad_gain_three = back_third(grad_normed)
     grad_after = cotangent.astype(jnp.float32) + grad_back
-    branch_after = grad_after.astype(jnp.bfloat16)
-    grad_crossed = project_back(branch_after, weights[7]).astype(jnp.bfloat16)
-    grad_cross_heads = split_heads(grad_crossed, head_count)
-    cross_all = (
-        lax.all_gather(cross_pair[0], "ctx", axis=1, tiled=True),
-        lax.all_gather(cross_pair[1], "ctx", axis=1, tiled=True),
-    )
-    cross_back = attend_back(
-        cross_queries, cross_heads, grad_cross_heads, cross_lse, cross_all, None, query_begin
-    )
-    cross_kv_sum = (
-        lax.psum_scatter(
-            cross_back[1].astype(jnp.bfloat16), "ctx", scatter_dimension=1, tiled=True
-        ).astype(jnp.float32),
-        lax.psum_scatter(
-            cross_back[2].astype(jnp.bfloat16), "ctx", scatter_dimension=1, tiled=True
-        ).astype(jnp.float32),
-    )
-    grad_cquery = join_heads(cross_back[0]).astype(jnp.bfloat16)
-    grad_ckeys = join_heads(cross_kv_sum[0]).astype(jnp.bfloat16)
-    grad_cvalues = join_heads(cross_kv_sum[1]).astype(jnp.bfloat16)
+    branch_after = grad_after.astype(low)
+    grad_crossed = project_back(branch_after, weights[7]).astype(low)
+    (cross_grads,) = spread([to_groups(grad_crossed, True)], [], 6)
+    cross_dq, cross_dkv = attend_back(cross_q, cross_kv, cross_grads, cross_full, cross_lse, None)
+    cross_dq, cross_dkv = collect(cross_dq, cross_dkv, 7)
+    grad_cquery = from_groups(cross_dq, 0)
+    grad_ckeys = from_groups(cross_dkv, 0)
+    grad_cvalues = from_groups(cross_dkv, 192)
     grad_encoder = project_back(grad_ckeys, weights[5]) + project_back(grad_cvalues, weights[6])
     grad_back, grad_gain_two = back_second(project_back(grad_cquery, weights[4]))
     grad_middle = grad_after + grad_back
-    branch_grad = grad_middle.astype(jnp.bfloat16)
-    grad_attended = project_back(branch_grad, weights[3]).astype(jnp.bfloat16)
-    grad_self_heads = split_heads(grad_attended, head_count)
-    self_all = (
-        lax.all_gather(self_pair[0], "ctx", axis=1, tiled=True),
-        lax.all_gather(self_pair[1], "ctx", axis=1, tiled=True),
+    branch_middle = grad_middle.astype(low)
+    grad_attended = project_back(branch_middle, weights[3]).astype(low)
+    (self_grads,) = spread([to_groups(grad_attended, True)], [], 8)
+    self_dq, self_dkv, grad_waves = attend_back(
+        self_q, self_kv, self_grads, self_full, self_lse, wide
     )
-    self_back = attend_back(
-        queries, self_heads, grad_self_heads, self_lse, self_all, bias_info, query_begin
-    )
-    self_kv_sum = (
-        lax.psum_scatter(
-            self_back[1].astype(jnp.bfloat16), "ctx", scatter_dimension=1, tiled=True
-        ).astype(jnp.float32),
-        lax.psum_scatter(
-            self_back[2].astype(jnp.bfloat16), "ctx", scatter_dimension=1, tiled=True
-        ).astype(jnp.float32),
-    )
-    grad_queries = join_heads(self_back[0]).astype(jnp.bfloat16)
-    grad_keys = join_heads(self_kv_sum[0]).astype(jnp.bfloat16)
-    grad_values = join_heads(self_kv_sum[1]).astype(jnp.bfloat16)
+    self_dq, self_dkv = collect(self_dq, self_dkv, 9)
+    grad_queries = from_groups(self_dq, 0)
+    grad_keys = from_groups(self_dkv, 0)
+    grad_values = from_groups(self_dkv, 192)
     grad_normed = (
         project_back(grad_queries, weights[0])
         + project_back(grad_keys, weights[1])
@@ -805,32 +1094,33 @@
     )
     grad_back, grad_gain_one = back_first(grad_normed)
     grad_input = grad_middle + grad_back
-    offset_grads = self_back[3][:, margin : margin + distance_count]
-    local_table = jnp.transpose(jnp.dot(offset_grads, table_hot, precision=PRECISE))
+    own_grads = jnp.einsum("kxb,hkx->bh", hot, grad_waves, precision=PRECISE)
+    local_table = lax.dynamic_update_slice_in_dim(
+        jnp.zeros_like(bias_table), own_grads, first_head, 1
+    )
     small = jnp.concatenate(
         [grad_gain_one, grad_gain_two, grad_gain_three, local_table.reshape(-1)]
     )
     small = jnp.pad(small, (0, 24 * 128 - small.shape[0])).reshape(24, 128)
     partials = outer_products(
-        jnp.concatenate(
+        jnp.stack(
             [normed_one, normed_one, normed_one, attended, normed_two, encoder_states, encoder_states, crossed]
         ),
-        jnp.concatenate(
-            [grad_queries, grad_keys, grad_values, branch_grad, grad_cquery, grad_ckeys, grad_cvalues, branch_after]
+        jnp.stack(
+            [grad_queries, grad_keys, grad_values, branch_middle, grad_cquery, grad_ckeys, grad_cvalues, branch_after]
         ),
-        normed_three[0],
-        grad_gate[0],
-        grad_up[0],
-        mixed_low[0],
-        cotangent[0],
+        normed_three,
+        grad_gate,
+        grad_up,
+        mixed_low,
+        cotangent,
     )
     *shards, sums = reduce_weights(partials, small, 1)
     sums = sums.reshape(-1)
-    width = model_width
     return (
-        layer_output,
-        grad_input,
-        grad_encoder,
+        layer_output[None],
+        grad_input[None],
+        grad_encoder[None],
         sums[3 * width : 3 * width + bucket_count * head_count].reshape(bucket_count, head_count),
         sums[:width],
         sums[width : 2 * width],

time: 1100 us -> 474 us (0.43)
  local copies, waits for them, and re-layouts: 395 us -> 56.1 us
  waiting for transfers between devices: 304 us -> 0 us
  Pallas kernels: 168 us -> 353 us
  matrix products: 149 us -> 33.7 us
  other arithmetic: 58.9 us -> 19.9 us
  between operations: 15.7 us -> 2.42 us
    unnamed x12 -> x0, waiting for transfers between devices: 215 us -> none
    pallas_call x0 -> x12, Pallas kernels: none -> 188 us  [the longest x4 70.3 us: collect(): pl.pallas_call(functools.partial(collect_kernel, with_kv), out_shape=shap...]
    dot_general x68 -> x24, matrix products: 149 us -> 33.7 us  [the longest x11 20.1 us: project_back(): jnp.einsum('tf,df->td', gradient, weight, preferred_element_type=jnp.floa...]
    reshape x13 -> x8, local copies, waits for them, and re-layouts: 110 us -> 5.83 us  [the longest x4 3.83 us: to_groups(): cut = activity.reshape(activity.shape[0], 4, 192).transpose(1, 0, 2)]
    all_gather x4 -> x0, waiting for transfers between devices: 89.2 us -> none  [the longest x1 44 us: body(): lax.all_gather(cross_pair[1], 'ctx', axis=1, tiled=True)]
    unnamed x184 -> x194, local copies, waits for them, and re-layouts: 114 us -> 26.2 us
    another operation x14 -> x11, local copies, waits for them, and re-layouts: 60.6 us -> 4.47 us  [the longest x3 3.51 us: body(): jnp.stack([normed_one, normed_one, normed_one, attended, normed_two, enco...]
    slice x13 -> x1, local copies, waits for them, and re-layouts: 46.4 us -> 1.1 us  [body(): padded[last - 255 - 128 * k - 0:last - 128 * k]]
  transfers between devices with their start and end apart: 8 -> 0, of which waited for: 6 -> 0; matrix products, arithmetic and copies ran while one was open for 18% -> 0% of each run, Pallas kernels for 0% -> 0%
where the time goes in v2:
time: 474 us; the launch traced here: 465 us
  Pallas kernels  353 us (74%)
  local copies, waits for them, and re-layouts  56.1 us (12%)
  matrix products  33.7 us (7%)
  other arithmetic  19.9 us (4%)
    pallas_call x1, Pallas kernels, reduce_weights(): pl.pallas_call(reduce_kernel, out_shape=[jax.ShapeDtypeStruct(shape, bf)...  83.7 us
    pallas_call x4, Pallas kernels, collect(): pl.pallas_call(functools.partial(collect_kernel, with_kv), out_shape=shap...  70.3 us
    pallas_call x1, Pallas kernels, gather_weights(): pl.pallas_call(functools.partial(gather_kernel, count, plan), out_shape=[...  67.6 us
    pallas_call x4, Pallas kernels, spread(): pl.pallas_call(functools.partial(spread_kernel, nq, nkv), out_shape=[jax....  63.6 us
    pallas_call x2, Pallas kernels, attend_back(): pl.pallas_call(functools.partial(backward_kernel, causal), out_shape=shap...  32.8 us
    unnamed x194, local copies, waits for them, and re-layouts  26.2 us
    pallas_call x2, Pallas kernels, attend(): pl.pallas_call(functools.partial(forward_kernel, causal), out_shape=shape...  21.2 us
    dot_general x11, matrix products, project_back(): jnp.einsum('tf,df->td', gradient, weight, preferred_element_type=jnp.floa...  20.1 us

profile of v2, /device:TPU:1, one launch (start us, length us, event | category | flops | bytes accessed | tf_op | source)
XLA Modules:
  0.0 465.0 jit_solution(13746765176867067761)
XLA Ops:
  3.0 67.6 %gather_weights.1 = (bf16[4,2,96,768]{3,2,1,0:T(8,128)(2,1)}, bf16[4,2,96,768]{3,2,1,0:T(8,128)(2,1)}, bf16[4,2,96,768]{3,2,1,0:T(8,128)(2,1)}, bf16[4,2,96,768]...) custom-call(bf16[96,768]{1,0:T(8,128)(2,1)} %refs_0_.1, ...), custom_call_target="tpu_custom_call" | custom-call | tf_op jit(solution)/shard_map/gather_weights/pallas_call | solution.py:186
  76.7 2.1 pad_maximum_fusion
  80.5 30.9 %spread_1_2.1 = (bf16[4,128,256]{2,1,0:T(8,128)(2,1)S(1)}, bf16[16,128,384]{2,1,0:T(8,128)(2,1)S(1)}, bf16[16,128,384]{2,1,0:T(8,128)(2,1)S(1)}) custom-call(bf16[4,128,256]{2,1,0:T(8,128)(2,1)S(1)} %pad.26.refs_0_, bf16[4,128,384]{2,1,0:T(8,128)(2,1)S(1)} %get-tuple-element.177.refs_1_, bf16[4,128,384]{2,1,0:T(8,128)(2,1)S(1)} %copy-done.11), custom_call_target="tpu_custom_call" | custom-call | tf_op jit(solution)/shard_map/spread_1_2/pallas_call | solution.py:621
  112.5 10.5 %attend_self.1 = (bf16[4,128,256]{2,1,0:T(8,128)(2,1)S(1)}, f32[4,128,256]{2,1,0:T(8,128)S(1)}, f32[3,2,1,256]{3,2,1,0:T(1,128)S(1)}, f32[3,2944,128]{2,1,0:T(8,128)S(1)}) custom-call(bf16[4,128,256]{2,1,0:T(8,128)(2,1)S(1)} %get-tuple-element.65.refs_0_, bf16[16,128,384]{2,1,0:T(8,128)(2,1)S(1)} %get-tuple-element.66.refs_1_, f32[3,23,256]{2,1,0:T(8,128)S(1)} %copy-done.21), custom_call_target="tpu_custom_call" | custom-call | tf_op jit(solution)/shard_map/attend_self/pallas_call | solution.py:835
  123.0 2.1 copy-done.2
  125.9 7.1 %collect.2 = bf16[4,128,256]{2,1,0:T(8,128)(2,1)S(1)} custom-call(bf16[4,128,256]{2,1,0:T(8,128)(2,1)S(1)} %get-tuple-element.67.refs_0_), custom_call_target="tpu_custom_call" | custom-call | tf_op jit(solution)/shard_map/collect/pallas_call | solution.py:725
  142.4 10.7 %spread_1_0.3.refs_0_ = bf16[4,128,256]{2,1,0:T(8,128)(2,1)S(1)} custom-call(bf16[4,128,256]{2,1,0:T(8,128)(2,1)S(1)} %pad.29.refs_0_), custom_call_target="tpu_custom_call" | custom-call | tf_op jit(solution)/shard_map/spread_1_0/pallas_call | solution.py:621
  153.1 10.7 %attend_cross.1 = (bf16[4,128,256]{2,1,0:T(8,128)(2,1)S(1)}, f32[4,128,256]{2,1,0:T(8,128)S(1)}, f32[3,2,1,256]{3,2,1,0:T(1,128)S(1)}) custom-call(bf16[4,128,256]{2,1,0:T(8,128)(2,1)S(1)} %spread_1_0.3.refs_0_, bf16[16,128,384]{2,1,0:T(8,128)(2,1)S(1)} %get-tuple-element.70.refs_1_), custom_call_target="tpu_custom_call" | custom-call | tf_op jit(solution)/shard_map/attend_cross/pallas_call | solution.py:835
  165.3 9.8 %collect.3 = bf16[4,128,256]{2,1,0:T(8,128)(2,1)S(1)} custom-call(bf16[4,128,256]{2,1,0:T(8,128)(2,1)S(1)} %get-tuple-element.71.refs_0_), custom_call_target="tpu_custom_call" | custom-call | tf_op jit(solution)/shard_map/collect/pallas_call | solution.py:725
  179.2 2.6 fusion.47
  184.0 2.4 multiply_convert_fusion
  197.8 11.8 %spread_1_0.4.refs_2_ = bf16[4,128,256]{2,1,0:T(8,128)(2,1)S(1)} custom-call(bf16[4,128,256]{2,1,0:T(8,128)(2,1)S(1)} %pad.30.refs_0_), custom_call_target="tpu_custom_call" | custom-call | tf_op jit(solution)/shard_map/spread_1_0/pallas_call | solution.py:621
  211.6 15.1 %attend_back_cross.1 = (bf16[4,128,256]{2,1,0:T(8,128)(2,1)S(1)}, bf16[16,128,384]{2,1,0:T(8,128)(2,1)S(1)}) custom-call(bf16[4,128,256]{2,1,0:T(8,128)(2,1)S(1)} %copy-done.4, bf16[16,128,384]{2,1,0:T(8,128)(2,1)S(1)} %get-tuple-element.70.refs_1_, bf16[4,128,256]{2,1,0:T(8,128)(2,1)S(1)} %spread_1_0.4.refs_2_, f32[4,128,256]{2,1,0:T(8,128)S(1)} %copy-done.20, ...), custom_call_target="tpu_custom_call" | custom-call | tf_op jit(solution)/shard_map/attend_back_cross/pallas_call | solution.py:944
  226.7 27.1 %collect_kv.2 = (bf16[4,128,256]{2,1,0:T(8,128)(2,1)S(1)}, bf16[4,128,384]{2,1,0:T(8,128)(2,1)S(1)}) custom-call(bf16[4,128,256]{2,1,0:T(8,128)(2,1)S(1)} %get-tuple-element.78.refs_0_, bf16[8,2,128,384]{3,2,1,0:T(8,128)(2,1)S(1)} %bitcast.193), custom_call_target="tpu_custom_call" | custom-call | tf_op jit(solution)/shard_map/collect_kv/pallas_call | solution.py:725
  254.8 2.0 multiply_reduce_fusion.1
  258.8 10.2 %spread_1_0.5.refs_2_ = bf16[4,128,256]{2,1,0:T(8,128)(2,1)S(1)} custom-call(bf16[4,128,256]{2,1,0:T(8,128)(2,1)S(1)} %pad.31.refs_0_), custom_call_target="tpu_custom_call" | custom-call | tf_op jit(solution)/shard_map/spread_1_0/pallas_call | solution.py:621
  271.0 17.8 %attend_back_self.1 = (bf16[4,128,256]{2,1,0:T(8,128)(2,1)S(1)}, bf16[16,128,384]{2,1,0:T(8,128)(2,1)S(1)}, f32[3,23,256]{2,1,0:T(8,128)S(1)}) custom-call(bf16[4,128,256]{2,1,0:T(8,128)(2,1)S(1)} %copy-done.13, bf16[16,128,384]{2,1,0:T(8,128)(2,1)S(1)} %get-tuple-element.66.refs_1_, bf16[4,128,256]{2,1,0:T(8,128)(2,1)S(1)} %spread_1_0.5.refs_2_, ...), custom_call_target="tpu_custom_call" | custom-call | tf_op jit(solution)/shard_map/attend_back_self/pallas_call | solution.py:944
  291.8 26.3 %collect_kv.3 = (bf16[4,128,256]{2,1,0:T(8,128)(2,1)S(1)}, bf16[4,128,384]{2,1,0:T(8,128)(2,1)S(1)}) custom-call(bf16[4,128,256]{2,1,0:T(8,128)(2,1)S(1)} %copy-done.23, bf16[8,2,128,384]{3,2,1,0:T(8,128)(2,1)S(1)} %bitcast.192), custom_call_target="tpu_custom_call" | custom-call | tf_op jit(solution)/shard_map/collect_kv/pallas_call | solution.py:725
  318.3 2.6 fusion.49
  323.1 2.3 convolution_add_fusion.2
  326.5 2.8 fusion.18
  349.3 13.6 %outer_products.1 = bf16[2,6,4,2,2,4,16,768]{7,6,5,4,3,2,1,0:T(8,128)(2,1)} custom-call(bf16[8,128,768]{2,1,0:T(8,128)(2,1)S(1)} %copy-done.10, bf16[8,128,768]{2,1,0:T(8,128)(2,1)S(1)} %bitcast_dynamic-update-slice_fusion.grads, bf16[128,768]{1,0:T(8,128)(2,1)S(1)} %multiply_convert_fusion.2.third, bf16[128,2048]{1,0:T(8,128)(2,1)S(1)} %copy-done.8, ...), custom_call_target="tpu_custom_call" | custom-call | tf_op jit(solution)/shard_map/outer_products/pallas_call | solution.py:471
  362.9 83.7 %reduce_weights.1 = (bf16[96,768]{1,0:T(8,128)(2,1)}, bf16[96,768]{1,0:T(8,128)(2,1)}, bf16[96,768]{1,0:T(8,128)(2,1)}, bf16[96,768]{1,0:T(8,128)(2,1)}, bf16[96...) custom-call(bf16[2,6,4,4,4,16,768]{6,5,4,3,2,1,0:T(8,128)(2,1)} %bit, ...), custom_call_target="tpu_custom_call" | custom-call | tf_op jit(solution)/shard_map/reduce_weights/pallas_call | solution.py:416
  446.6 2.0 convert_element_type.152
  (295 shorter events, 88.7 us)
Async XLA Ops:
  0.7 69.9 %copy-start.24 = (bf16[1,128,768]{2,1,0:T(8,128)(2,1)S(1)}, bf16[1,128,768]{2,1,0:T(8,128)(2,1)}, u32[]{:S(2)}) copy-start(bf16[1,128,768]{2,1,0:T(8,128)(2,1)} %param.19) | copy-start | bytes 589828
  0.7 70.6 %copy-start.63 = (f32[768]{0:T(1024)S(1)}, f32[768]{0:T(1024)}, u32[]{:S(2)}) copy-start(f32[768]{0:T(1024)} %param.24) | copy-start | bytes 9220
  2.0 68.8 %copy-start.79 = (s32[23,256]{1,0:T(8,128)}, s32[23,256]{1,0:T(8,128)S(1)}, u32[]{:S(2)}) copy-start(s32[23,256]{1,0:T(8,128)S(1)} %pad.28) | copy-start | bytes 70660
  71.3 7.5 %copy-start.77 = (f32[128]{0:T(128)}, f32[128]{0:T(128)S(1)}, u32[]{:S(2)}) copy-start(f32[128]{0:T(128)S(1)} %fusion.39) | copy-start | bytes 1540
  111.5 11.5 %copy-start.12 = (bf16[4,128,256]{2,1,0:T(8,128)(2,1)}, bf16[4,128,256]{2,1,0:T(8,128)(2,1)S(1)}, u32[]{:S(2)}) copy-start(bf16[4,128,256]{2,1,0:T(8,128)(2,1)S(1)} %get-tuple-element.65.refs_0_) | copy-start | bytes 786436
  135.8 5.6 %copy-start.27 = (f32[128,768]{1,0:T(8,128)}, f32[128,768]{1,0:T(8,128)S(1)}, u32[]{:S(2)}) copy-start(f32[128,768]{1,0:T(8,128)S(1)} %get-tuple-element.171) | copy-start | bytes 1179652
  179.0 11.5 %copy-start.31 = (f32[128,768]{1,0:T(8,128)}, f32[128,768]{1,0:T(8,128)S(1)}, u32[]{:S(2)}) copy-start(f32[128,768]{1,0:T(8,128)S(1)} %get-tuple-element.173) | copy-start | bytes 1179652
  226.7 28.1 %copy-start.28 = (f32[128,768]{1,0:T(8,128)S(1)}, f32[128,768]{1,0:T(8,128)}, u32[]{:S(2)}) copy-start(f32[128,768]{1,0:T(8,128)} %copy-done.27) | copy-start | bytes 1179652
  226.7 28.1 %copy-start.74 = (f32[768]{0:T(1024)S(1)}, f32[768]{0:T(1024)}, u32[]{:S(2)}) copy-start(f32[768]{0:T(1024)} %param.25) | copy-start | bytes 9220
  226.7 28.1 %copy-start.85 = (f32[128]{0:T(128)S(1)}, f32[128]{0:T(128)}, u32[]{:S(2)}) copy-start(f32[128]{0:T(128)} %copy-done.84) | copy-start | bytes 1540
  271.0 18.5 %copy-start.80 = (s32[23,256]{1,0:T(8,128)S(1)}, s32[23,256]{1,0:T(8,128)}, u32[]{:S(2)}) copy-start(s32[23,256]{1,0:T(8,128)} %copy-done.79) | copy-start | bytes 70660
  318.3 4.8 %copy-start.44 = (bf16[4,2,96,768]{3,2,1,0:T(8,128)(2,1)S(1)}, bf16[4,2,96,768]{3,2,1,0:T(8,128)(2,1)}, u32[]{:S(2)}) copy-start(bf16[4,2,96,768]{3,2,1,0:T(8,128)(2,1)} %get-tuple-element.61) | copy-start | bytes 3538948
  321.8 4.7 %copy-start.25 = (bf16[1,128,768]{2,1,0:T(8,128)(2,1)S(1)}, bf16[1,128,768]{2,1,0:T(8,128)(2,1)}, u32[]{:S(2)}) copy-start(bf16[1,128,768]{2,1,0:T(8,128)(2,1)} %param.19) | copy-start | bytes 589828
  321.8 4.7 %copy-start.42 = (bf16[4,2,96,768]{3,2,1,0:T(8,128)(2,1)S(1)}, bf16[4,2,96,768]{3,2,1,0:T(8,128)(2,1)}, u32[]{:S(2)}) copy-start(bf16[4,2,96,768]{3,2,1,0:T(8,128)(2,1)} %get-tuple-element.62) | copy-start | bytes 3538948
  321.8 4.7 %copy-start.64 = (f32[768]{0:T(1024)S(1)}, f32[768]{0:T(1024)}, u32[]{:S(2)}) copy-start(f32[768]{0:T(1024)} %param.24) | copy-start | bytes 9220
  321.8 4.7 %copy-start.78 = (f32[128]{0:T(128)S(1)}, f32[128]{0:T(128)}, u32[]{:S(2)}) copy-start(f32[128]{0:T(128)} %copy-done.77) | copy-start | bytes 1540
  332.0 5.4 %copy-start.86 = (f32[128]{0:T(128)S(1)}, f32[128]{0:T(128)}, u32[]{:S(2)}) copy-start(f32[128]{0:T(128)} %copy-done.84) | copy-start | bytes 1540
  446.6 5.0 %copy-start.72 = (bf16[96,768]{1,0:T(8,128)(2,1)S(1)}, bf16[96,768]{1,0:T(8,128)(2,1)}, u32[]{:S(2)}) copy-start(bf16[96,768]{1,0:T(8,128)(2,1)} %get-tuple-element.91) | copy-start | bytes 442372
  448.6 5.2 %copy-start.69 = (bf16[96,768]{1,0:T(8,128)(2,1)S(1)}, bf16[96,768]{1,0:T(8,128)(2,1)}, u32[]{:S(2)}) copy-start(bf16[96,768]{1,0:T(8,128)(2,1)} %get-tuple-element.94) | copy-start | bytes 442372
  451.6 5.2 %copy-start.65 = (bf16[96,768]{1,0:T(8,128)(2,1)S(1)}, bf16[96,768]{1,0:T(8,128)(2,1)}, u32[]{:S(2)}) copy-start(bf16[96,768]{1,0:T(8,128)(2,1)} %get-tuple-element.98) | copy-start | bytes 442372
  452.3 5.2 %copy-start.81 = (f32[24,128]{1,0:T(8,128)S(1)}, f32[24,128]{1,0:T(8,128)}, u32[]{:S(2)}) copy-start(f32[24,128]{1,0:T(8,128)} %get-tuple-element.90) | copy-start | bytes 36868
  452.3 6.6 %copy-start.56 = (bf16[128,4,192]{0,2,1:T(8,128)(2,1)S(1)}, bf16[128,4,192]{0,2,1:T(8,128)(2,1)}, u32[]{:S(2)}) copy-start(bf16[128,4,192]{0,2,1:T(8,128)(2,1)} %copy-done.55) | copy-start | bytes 589828
  455.3 5.6 %copy-start.40 = (bf16[4,2,96,768]{3,2,1,0:T(8,128)(2,1)S(1)}, bf16[4,2,96,768]{3,2,1,0:T(8,128)(2,1)}, u32[]{:S(2)}) copy-start(bf16[4,2,96,768]{3,2,1,0:T(8,128)(2,1)} %get-tuple-element.64) | copy-start | bytes 3538948
  455.3 5.6 %copy-start.58 = (bf16[128,4,192]{0,2,1:T(8,128)(2,1)S(1)}, bf16[128,4,192]{0,2,1:T(8,128)(2,1)}, u32[]{:S(2)}) copy-start(bf16[128,4,192]{0,2,1:T(8,128)(2,1)} %copy-done.57) | copy-start | bytes 589828
  (68 other events, 142.4 us)
